TPU v7x, 32 devices: a whole 2x2x4 slice. The times are simulated.
32 devices in a mesh: head: 2 (over y), inner: 2 (over x), outer: 8 (over z, core).
Axes of the slice: x: 2, y: 2, z: 4, core: 2. Of those that a mesh axis runs over, the one named last changes fastest.
Arguments:
- query_nope: bfloat16 [2048, 8192], P(('inner', 'outer'), 'head'), may hold values from -6 to 6
- query_rope: bfloat16 [2048, 4096], P(('inner', 'outer'), 'head'), may hold values from -256 to 256
- latent: bfloat16 [2048, 512], P(('inner', 'outer')), may hold values from -6 to 6
- key_rope: bfloat16 [2048, 64], P(('inner', 'outer')), may hold values from -4 to 4
- key_up: bfloat16 [512, 8192], P(None, 'head'), may hold values from -0.25 to 0.25
- value_up: bfloat16 [512, 8192], P(None, 'head'), may hold values from -0.25 to 0.25
- latent_out: bfloat16 [2048, 32768], P(('inner', 'outer'), 'head'), may hold values from -3 to 3
- out_grad: bfloat16 [2048, 8192], P(('inner', 'outer'), 'head'), may hold values from -6 to 6
- logsum: float32 [2048, 64], P(('inner', 'outer'), 'head'), may hold values from 0 to 5000
- block_order: int32 [32], replicated, may hold values from 0 to 31, as said below
Outputs:
- d_query_nope: bfloat16 [2048, 8192], P(('inner', 'outer'), 'head')
- d_query_rope: bfloat16 [2048, 4096], P(('inner', 'outer'), 'head')
- d_latent: bfloat16 [2048, 512], P(('inner', 'outer'))
- d_key_rope: bfloat16 [2048, 64], P(('inner', 'outer'))
- d_key_up: float32 [512, 8192], P(('inner', 'outer'), 'head')
- d_value_up: float32 [512, 8192], P(('inner', 'outer'), 'head')
Inputs may be any that keep to these rules, and one draw needn't show every extreme that they name: `block_order`: stored blocks 2 r and 2 r + 1 hold sequence blocks c and 31 - c for some c, in either order; every sequence block is held once.
All inputs are finite; a program needn't handle non-finite values.
Results may differ from a plain program's by a relative error of at most 0.0085.
The roundings to bfloat16 on the way count: a program that leaves them out, or rounds other values in their place, can miss the bound.
Values may be sent and summed in bfloat16 or wider, within the bound.
A program may use at most 128 MiB of HBM per device.

v0:
```python
import functools

import jax
import jax.numpy as jnp
from jax import lax
from jax.sharding import PartitionSpec as P

LATENT = 512
ROPE_DIM = 64
NOPE_DIM = 128
VALUE_DIM = 128


def shifted(block, axis, distance):
    devices = range(lax.axis_size(axis))
    route = [((i - distance) % len(devices), i) for i in devices]
    return lax.ppermute(block, axis, route)


def key_positions(block_order, first_row, length, block_size):
    indices = first_row + lax.iota(jnp.int32, length)
    owners = indices // block_size
    lookup = lax.iota(jnp.int32, block_order.shape[0])
    picked = (owners[:, None] == lookup[None, :]).astype(jnp.int32)
    return jnp.sum(picked * block_order[None, :], axis=1) * block_size + indices % block_size


def contract_last(first_op, second_op):
    return lax.dot_general(
        first_op, second_op, (((1,), (1,)), ((), ())), preferred_element_type=jnp.float32
    )


def contract_first(first_op, second_op):
    return lax.dot_general(
        first_op, second_op, (((0,), (0,)), ((), ())), preferred_element_type=jnp.float32
    )


def scaled_scores(queries, lat_keys, rope_keys):
    factor = float(NOPE_DIM + ROPE_DIM) ** (-0.5)
    return (contract_last(lat_keys, queries[0]) + contract_last(rope_keys, queries[1])) * factor


def unchanged(current):
    return current


def grad_update(carried, queries, lat_keys, rope_keys, positions):
    factor = float(NOPE_DIM + ROPE_DIM) ** (-0.5)
    scores = scaled_scores(queries, lat_keys, rope_keys)
    visible = positions[:, None] <= queries[2][None, :]
    weights = jnp.where(
        visible, jnp.exp(jnp.where(visible, scores - queries[5][None, :], 0.0)), 0.0
    )
    dprobs = contract_last(lat_keys, queries[3])
    dscore = (weights * (dprobs - queries[4][None, :]) * factor).astype(jnp.bfloat16)
    rounded = weights.astype(jnp.bfloat16)
    return (
        carried[0] + contract_first(dscore, lat_keys),
        carried[1] + contract_first(dscore, rope_keys),
        carried[2]
        + jnp.dot(dscore, queries[0], preferred_element_type=jnp.float32)
        + jnp.dot(rounded, queries[3], preferred_element_type=jnp.float32),
        carried[3] + jnp.dot(dscore, queries[1], preferred_element_type=jnp.float32),
    )


def single_block(carried, queries, lat_keys, rope_keys, positions, offset, block_size):
    part_lat = lax.dynamic_slice_in_dim(lat_keys, offset, block_size, 0)
    part_rope = lax.dynamic_slice_in_dim(rope_keys, offset, block_size, 0)
    part_pos = lax.dynamic_slice_in_dim(positions, offset, block_size, 0)
    sum_lat = lax.dynamic_slice_in_dim(carried[2], offset, block_size, 0)
    sum_rope = lax.dynamic_slice_in_dim(carried[3], offset, block_size, 0)
    result = grad_update(
        (carried[0], carried[1], sum_lat, sum_rope), queries, part_lat, part_rope, part_pos
    )
    return (
        result[0],
        result[1],
        lax.dynamic_update_slice_in_dim(carried[2], result[2], offset, 0),
        lax.dynamic_update_slice_in_dim(carried[3], result[3], offset, 0),
    )


def shard_grads(query_pairs, query_grads, lat_keys, rope_keys, positions):
    block_size = lat_keys.shape[0] // 2
    key_lat = jnp.zeros(lat_keys.shape, jnp.float32)
    key_rope_acc = jnp.zeros(rope_keys.shape, jnp.float32)
    updated = []
    for target in range(2):
        queries = query_pairs[target]
        latest = queries[2][-1]
        first_seen = positions[0] <= latest
        second_seen = positions[block_size] <= latest
        branch_index = first_seen.astype(jnp.int32) + second_seen.astype(jnp.int32)
        offset = jnp.where(first_seen, 0, block_size).astype(jnp.int32)
        whole = functools.partial(
            grad_update,
            queries=queries,
            lat_keys=lat_keys,
            rope_keys=rope_keys,
            positions=positions,
        )
        single = functools.partial(
            single_block,
            queries=queries,
            lat_keys=lat_keys,
            rope_keys=rope_keys,
            positions=positions,
            offset=offset,
            block_size=block_size,
        )
        carried = lax.switch(
            branch_index,
            [unchanged, single, whole],
            (query_grads[target][0], query_grads[target][1], key_lat, key_rope_acc),
        )
        updated.append((carried[0], carried[1]))
        key_lat, key_rope_acc = (carried[2], carried[3])
    return (tuple(updated), (key_lat, key_rope_acc))


def local(
    query_nope,
    query_rope,
    latent,
    key_rope,
    key_up,
    value_up,
    latent_out,
    out_grad,
    logsum,
    block_order,
):
    tokens = query_nope.shape[0]
    head_count = query_nope.shape[1] // NOPE_DIM
    block_size = tokens // 2
    flat_rows = block_size * head_count
    nope_heads = query_nope.reshape(tokens, head_count, NOPE_DIM)
    rope_heads = query_rope.reshape(tokens, head_count, ROPE_DIM)
    saved = latent_out.reshape(tokens, head_count, LATENT)
    upstream = out_grad.reshape(tokens, head_count, VALUE_DIM)
    key_map = key_up.reshape(LATENT, head_count, NOPE_DIM)
    value_map = value_up.reshape(LATENT, head_count, VALUE_DIM)
    query_latent = jnp.einsum(
        "thn,lhn->thl", nope_heads, key_map, preferred_element_type=jnp.float32
    ).astype(jnp.bfloat16)
    grad_latent = jnp.einsum(
        "thv,lhv->thl", upstream, value_map, preferred_element_type=jnp.float32
    ).astype(jnp.bfloat16)
    row_delta = jnp.sum(grad_latent.astype(jnp.float32) * saved.astype(jnp.float32), axis=2)
    context_size = lax.axis_size(("inner", "outer"))
    my_index = lax.axis_index(("inner", "outer"))
    own_positions = key_positions(block_order, my_index * tokens, tokens, block_size)
    query_parts = []
    for target in range(2):
        offset = target * block_size
        positions = jnp.broadcast_to(
            own_positions[offset : offset + block_size, None], (block_size, head_count)
        ).reshape(flat_rows)
        lat_part = query_latent[offset : offset + block_size].reshape(flat_rows, LATENT)
        rope_part = rope_heads[offset : offset + block_size].reshape(flat_rows, ROPE_DIM)
        grad_part = grad_latent[offset : offset + block_size].reshape(flat_rows, LATENT)
        delta_part = row_delta[offset : offset + block_size].reshape(flat_rows)
        total_part = logsum[offset : offset + block_size].reshape(flat_rows)
        query_parts.append((lat_part, rope_part, positions, grad_part, delta_part, total_part))
    backward_pairs = tuple(query_parts)
    zero_grads = tuple(
        (
            (
                jnp.zeros((flat_rows, LATENT), jnp.float32),
                jnp.zeros((flat_rows, ROPE_DIM), jnp.float32),
            )
            for target in range(2)
        )
    )

    def step_pair(turn_index, status):
        travelling, key_sums, query_grads = status
        for member in range(2):
            source = (my_index - 2 * turn_index - member) % context_size
            positions = key_positions(block_order, source * tokens, tokens, block_size)
            query_grads, contribution = shard_grads(
                backward_pairs, query_grads, travelling[0], travelling[1], positions
            )
            key_sums = (key_sums[0] + contribution[0], key_sums[1] + contribution[1])
            travelling = shifted((travelling[0], travelling[1]), ("inner", "outer"), 1)
            key_sums = shifted((key_sums[0], key_sums[1]), ("inner", "outer"), 1)
        return (travelling, key_sums, query_grads)

    start_sums = (
        jnp.zeros((tokens, LATENT), jnp.float32),
        jnp.zeros((tokens, ROPE_DIM), jnp.float32),
    )
    final_state = lax.fori_loop(
        0, context_size // 2, step_pair, ((latent, key_rope), start_sums, zero_grads)
    )
    own_sums = final_state[1]
    query_grads = final_state[2]
    summed = lax.psum((own_sums[0], own_sums[1]), "head")
    grad_query = jnp.concatenate([query_grads[0][0], query_grads[1][0]], axis=0)
    grad_query = grad_query.reshape(tokens, head_count, LATENT).astype(jnp.bfloat16)
    grad_rope = jnp.concatenate([query_grads[0][1], query_grads[1][1]], axis=0)
    d_query_rope = grad_rope.reshape(tokens, head_count * ROPE_DIM).astype(jnp.bfloat16)
    d_query_nope = jnp.einsum(
        "thl,lhn->thn", grad_query, key_map, preferred_element_type=jnp.float32
    )
    d_query_nope = d_query_nope.reshape(tokens, head_count * NOPE_DIM).astype(jnp.bfloat16)
    key_weight = jnp.einsum(
        "thl,thn->lhn", grad_query, nope_heads, preferred_element_type=jnp.float32
    )
    value_weight = jnp.einsum("thl,thv->lhv", saved, upstream, preferred_element_type=jnp.float32)
    weight_parts = (
        lax.psum_scatter(
            key_weight.reshape(LATENT, head_count * NOPE_DIM),
            ("inner", "outer"),
            scatter_dimension=0,
            tiled=True,
        ),
        lax.psum_scatter(
            value_weight.reshape(LATENT, head_count * VALUE_DIM),
            ("inner", "outer"),
            scatter_dimension=0,
            tiled=True,
        ),
    )
    return (
        d_query_nope,
        d_query_rope,
        summed[0].astype(jnp.bfloat16),
        summed[1].astype(jnp.bfloat16),
        weight_parts[0],
        weight_parts[1],
    )


def solution(mesh):
    placed = (
        P(("inner", "outer"), "head"),
        P(("inner", "outer"), "head"),
        P(("inner", "outer"), None),
        P(("inner", "outer"), None),
        P(None, "head"),
        P(None, "head"),
        P(("inner", "outer"), "head"),
        P(("inner", "outer"), "head"),
        P(("inner", "outer"), "head"),
        P(),
    )
    return jax.shard_map(
        local,
        mesh=mesh,
        in_specs=placed,
        out_specs=(
            P(("inner", "outer"), "head"),
            P(("inner", "outer"), "head"),
            P(("inner", "outer"), None),
            P(("inner", "outer"), None),
            P(("inner", "outer"), "head"),
            P(("inner", "outer"), "head"),
        ),
        check_vma=False,
    )
```

profile of v0, /device:TPU:0, one launch (start us, length us, event | category | flops | bytes accessed | tf_op | source)
XLA Modules:
  0.0 1143.4 jit_solution(6123727457917229146)
XLA Ops:
  10.4 6.7 copy.85
  17.2 6.7 fusion.159
  23.9 9.0 copy.101
  46.2 7.0 copy.106
  82.6 927.1 %while.31 = (s32[]{:T(128)}, bf16[128,512]{1,0:T(8,128)(2,1)}, bf16[128,64]{1,0:T(8,128)(2,1)}, f32[128,512]{1,0:T(8,128)}, f32[128,64]{0,1:T(8,128)}, /*index=5...) while((s32[]{:T(128)}, bf16[128,512]{1,0:T(8,128)(2,1)}, ...), condition=%wide.region_17.18_spmd.clone, body=%wide.region_2.17_spmd.clone.sunk | while | flops 5788204032 | bytes 167503920 | solution.py:196
  111.2 18.4 %conditional.12 = (f32[2048,512]{1,0:T(8,128)}, f32[2048,64]{0,1:T(8,128)}, f32[128,512]{1,0:T(8,128)}, f32[128,64]{0,1:T(8,128)}) conditional(s32[]{:T(128)} %clamp.53, (f32[2048,512]{1,0:T(8,128)}, f32[2048,64]{0,1:T(8,128)}) %tuple.143, (pred[]{:T(512)}, s32[128]{0:T(128)S(1)}, s32[64,32]{1,0:T(8,128)}, ...), branch_computations={%region_4.4_spmd, %region_5.5_spmd, %region_6.6_spmd} | conditional | flops 1446969344 | bytes 44311128 | solution.py:114
  130.8 19.7 %conditional.13 = ((f32[2048,512]{1,0:T(8,128)}, f32[2048,64]{0,1:T(8,128)}, f32[128,512]{1,0:T(8,128)}, f32[128,64]{0,1:T(8,128)})) conditional(s32[]{:T(128)} %clamp.52, (f32[2048,512]{1,0:T(8,128)}, f32[2048,64]{0,1:T(8,128)}, f32[128,512]{1,0:T(8,128)}, f32[128,64]{0,1:T(8,128)}) %tuple.146, (pred[]{:T(512)}, s32[128]{0:T(128)S(1)}, ...), branch_computations={%region_7.7_spmd, %region_8.8_spmd, %region_9.9_spmd} | conditional | flops 1447043072 | bytes 36217412 | solution.py:114
  158.7 19.0 %conditional.14 = (f32[2048,512]{1,0:T(8,128)}, f32[2048,64]{0,1:T(8,128)}, f32[128,512]{1,0:T(8,128)}, f32[128,64]{0,1:T(8,128)}) conditional(s32[]{:T(128)} %clamp.55, (f32[2048,512]{1,0:T(8,128)}, f32[2048,64]{0,1:T(8,128)}) %tuple.149, (pred[]{:T(512)}, s32[128]{0:T(128)S(1)}, s32[64,32]{1,0:T(8,128)}, ...), branch_computations={%region_11.11_spmd, %region_12.12_spmd, %region_13.13_spmd} | conditional | flops 1446969344 | bytes 44311128 | solution.py:114
  177.6 15.7 %conditional.15 = ((f32[2048,512]{1,0:T(8,128)}, f32[2048,64]{0,1:T(8,128)}, f32[128,512]{1,0:T(8,128)}, f32[128,64]{0,1:T(8,128)})) conditional(s32[]{:T(128)} %clamp.54, (f32[2048,512]{1,0:T(8,128)}, f32[2048,64]{0,1:T(8,128)}, f32[128,512]{1,0:T(8,128)}, f32[128,64]{0,1:T(8,128)}) %tuple.152, (pred[]{:T(512)}, ...), branch_computations={%region_14.14_spmd, %region_15.15_spmd, %region_16.16_spmd} | conditional | flops 1447043072 | bytes 36217412 | solution.py:114
  198.9 6.7 collective-permute-done.6
  224.8 18.3 %conditional.12 = (f32[2048,512]{1,0:T(8,128)}, f32[2048,64]{0,1:T(8,128)}, f32[128,512]{1,0:T(8,128)}, f32[128,64]{0,1:T(8,128)}) conditional(s32[]{:T(128)} %clamp.53, (f32[2048,512]{1,0:T(8,128)}, f32[2048,64]{0,1:T(8,128)}) %tuple.143, (pred[]{:T(512)}, s32[128]{0:T(128)S(1)}, s32[64,32]{1,0:T(8,128)}, ...), branch_computations={%region_4.4_spmd, %region_5.5_spmd, %region_6.6_spmd} | conditional | flops 1446969344 | bytes 44311128 | solution.py:114
  246.1 19.5 %collective-permute-start.4 = (f32[128,512]{1,0:T(8,128)}, f32[128,512]{1,0:T(8,128)}, u32[]{:S(2)}, u32[]{:S(2)}) collective-permute-start(f32[128,512]{1,0:T(8,128)} %add.732), channel_id=1, source_target_pairs={{15,0},{0,1},{1,2},{2,3},{3,4},{4,5},{5,6},{6,7},{7,8},{8,9},{9,10... | collective-permute-start | bytes 786440 | tf_op jit(solution)/shard_map/while/body/eval_jaxpr/ppermute | solution.py:17
  272.0 18.9 %conditional.14 = (f32[2048,512]{1,0:T(8,128)}, f32[2048,64]{0,1:T(8,128)}, f32[128,512]{1,0:T(8,128)}, f32[128,64]{0,1:T(8,128)}) conditional(s32[]{:T(128)} %clamp.55, (f32[2048,512]{1,0:T(8,128)}, f32[2048,64]{0,1:T(8,128)}) %tuple.149, (pred[]{:T(512)}, s32[128]{0:T(128)S(1)}, s32[64,32]{1,0:T(8,128)}, ...), branch_computations={%region_11.11_spmd, %region_12.12_spmd, %region_13.13_spmd} | conditional | flops 1446969344 | bytes 44311128 | solution.py:114
  290.9 15.7 %conditional.15 = ((f32[2048,512]{1,0:T(8,128)}, f32[2048,64]{0,1:T(8,128)}, f32[128,512]{1,0:T(8,128)}, f32[128,64]{0,1:T(8,128)})) conditional(s32[]{:T(128)} %clamp.54, (f32[2048,512]{1,0:T(8,128)}, f32[2048,64]{0,1:T(8,128)}, f32[128,512]{1,0:T(8,128)}, f32[128,64]{0,1:T(8,128)}) %tuple.152, (pred[]{:T(512)}, ...), branch_computations={%region_14.14_spmd, %region_15.15_spmd, %region_16.16_spmd} | conditional | flops 1447043072 | bytes 36217412 | solution.py:114
  311.0 7.8 collective-permute-done.6
  320.2 6.7 collective-permute-done.3
  337.9 18.3 %conditional.12 = (f32[2048,512]{1,0:T(8,128)}, f32[2048,64]{0,1:T(8,128)}, f32[128,512]{1,0:T(8,128)}, f32[128,64]{0,1:T(8,128)}) conditional(s32[]{:T(128)} %clamp.53, (f32[2048,512]{1,0:T(8,128)}, f32[2048,64]{0,1:T(8,128)}) %tuple.143, (pred[]{:T(512)}, s32[128]{0:T(128)S(1)}, s32[64,32]{1,0:T(8,128)}, ...), branch_computations={%region_4.4_spmd, %region_5.5_spmd, %region_6.6_spmd} | conditional | flops 1446969344 | bytes 44311128 | solution.py:114
  359.3 21.1 %collective-permute-start.4 = (f32[128,512]{1,0:T(8,128)}, f32[128,512]{1,0:T(8,128)}, u32[]{:S(2)}, u32[]{:S(2)}) collective-permute-start(f32[128,512]{1,0:T(8,128)} %add.732), channel_id=1, source_target_pairs={{15,0},{0,1},{1,2},{2,3},{3,4},{4,5},{5,6},{6,7},{7,8},{8,9},{9,10... | collective-permute-start | bytes 786440 | tf_op jit(solution)/shard_map/while/body/eval_jaxpr/ppermute | solution.py:17
  386.8 17.9 %conditional.14 = (f32[2048,512]{1,0:T(8,128)}, f32[2048,64]{0,1:T(8,128)}, f32[128,512]{1,0:T(8,128)}, f32[128,64]{0,1:T(8,128)}) conditional(s32[]{:T(128)} %clamp.55, (f32[2048,512]{1,0:T(8,128)}, f32[2048,64]{0,1:T(8,128)}) %tuple.149, (pred[]{:T(512)}, s32[128]{0:T(128)S(1)}, s32[64,32]{1,0:T(8,128)}, ...), branch_computations={%region_11.11_spmd, %region_12.12_spmd, %region_13.13_spmd} | conditional | flops 1446969344 | bytes 44311128 | solution.py:114
  408.9 16.7 %collective-permute-start.1 = (bf16[128,512]{1,0:T(8,128)(2,1)S(1)}, bf16[128,512]{1,0:T(8,128)(2,1)}, u32[]{:S(2)}, u32[]{:S(2)}) collective-permute-start(bf16[128,512]{1,0:T(8,128)(2,1)S(1)} %collective-permute-done), channel_id=1, source_target_pairs={{15,0},{0,1},{1,2},{2,3},{3,4},{4,5},{5,6},{6,7},{7,8},{8,9},{9,10... | collective-permute-start | bytes 393224 | tf_op jit(solution)/shard_map/while/body/eval_jaxpr/ppermute | solution.py:17
  451.6 18.3 %conditional.12 = (f32[2048,512]{1,0:T(8,128)}, f32[2048,64]{0,1:T(8,128)}, f32[128,512]{1,0:T(8,128)}, f32[128,64]{0,1:T(8,128)}) conditional(s32[]{:T(128)} %clamp.53, (f32[2048,512]{1,0:T(8,128)}, f32[2048,64]{0,1:T(8,128)}) %tuple.143, (pred[]{:T(512)}, s32[128]{0:T(128)S(1)}, s32[64,32]{1,0:T(8,128)}, ...), branch_computations={%region_4.4_spmd, %region_5.5_spmd, %region_6.6_spmd} | conditional | flops 1446969344 | bytes 44311128 | solution.py:114
  479.3 18.9 %conditional.14 = (f32[2048,512]{1,0:T(8,128)}, f32[2048,64]{0,1:T(8,128)}, f32[128,512]{1,0:T(8,128)}, f32[128,64]{0,1:T(8,128)}) conditional(s32[]{:T(128)} %clamp.55, (f32[2048,512]{1,0:T(8,128)}, f32[2048,64]{0,1:T(8,128)}) %tuple.149, (pred[]{:T(512)}, s32[128]{0:T(128)S(1)}, s32[64,32]{1,0:T(8,128)}, ...), branch_computations={%region_11.11_spmd, %region_12.12_spmd, %region_13.13_spmd} | conditional | flops 1446969344 | bytes 44311128 | solution.py:114
  498.2 15.7 %conditional.15 = ((f32[2048,512]{1,0:T(8,128)}, f32[2048,64]{0,1:T(8,128)}, f32[128,512]{1,0:T(8,128)}, f32[128,64]{0,1:T(8,128)})) conditional(s32[]{:T(128)} %clamp.54, (f32[2048,512]{1,0:T(8,128)}, f32[2048,64]{0,1:T(8,128)}, f32[128,512]{1,0:T(8,128)}, f32[128,64]{0,1:T(8,128)}) %tuple.152, (pred[]{:T(512)}, ...), branch_computations={%region_14.14_spmd, %region_15.15_spmd, %region_16.16_spmd} | conditional | flops 1447043072 | bytes 36217412 | solution.py:114
  527.5 14.4 %collective-permute-start.7 = (f32[128,64]{0,1:T(8,128)}, f32[128,64]{0,1:T(8,128)}, u32[]{:S(2)}, u32[]{:S(2)}) collective-permute-start(f32[128,64]{0,1:T(8,128)} %add.737), channel_id=1, source_target_pairs={{15,0},{0,1},{1,2},{2,3},{3,4},{4,5},{5,6},{6,7},{7,8},{8,9},{9,10... | collective-permute-start | bytes 98312 | tf_op jit(solution)/shard_map/while/body/eval_jaxpr/ppermute | solution.py:17
  562.3 18.3 %conditional.12 = (f32[2048,512]{1,0:T(8,128)}, f32[2048,64]{0,1:T(8,128)}, f32[128,512]{1,0:T(8,128)}, f32[128,64]{0,1:T(8,128)}) conditional(s32[]{:T(128)} %clamp.53, (f32[2048,512]{1,0:T(8,128)}, f32[2048,64]{0,1:T(8,128)}) %tuple.143, (pred[]{:T(512)}, s32[128]{0:T(128)S(1)}, s32[64,32]{1,0:T(8,128)}, ...), branch_computations={%region_4.4_spmd, %region_5.5_spmd, %region_6.6_spmd} | conditional | flops 1446969344 | bytes 44311128 | solution.py:114
  583.6 22.4 %collective-permute-start.4 = (f32[128,512]{1,0:T(8,128)}, f32[128,512]{1,0:T(8,128)}, u32[]{:S(2)}, u32[]{:S(2)}) collective-permute-start(f32[128,512]{1,0:T(8,128)} %add.732), channel_id=1, source_target_pairs={{15,0},{0,1},{1,2},{2,3},{3,4},{4,5},{5,6},{6,7},{7,8},{8,9},{9,10... | collective-permute-start | bytes 786440 | tf_op jit(solution)/shard_map/while/body/eval_jaxpr/ppermute | solution.py:17
  612.4 17.9 %conditional.14 = (f32[2048,512]{1,0:T(8,128)}, f32[2048,64]{0,1:T(8,128)}, f32[128,512]{1,0:T(8,128)}, f32[128,64]{0,1:T(8,128)}) conditional(s32[]{:T(128)} %clamp.55, (f32[2048,512]{1,0:T(8,128)}, f32[2048,64]{0,1:T(8,128)}) %tuple.149, (pred[]{:T(512)}, s32[128]{0:T(128)S(1)}, s32[64,32]{1,0:T(8,128)}, ...), branch_computations={%region_11.11_spmd, %region_12.12_spmd, %region_13.13_spmd} | conditional | flops 1446969344 | bytes 44311128 | solution.py:114
  632.0 16.7 %collective-permute-start.5 = (f32[128,512]{1,0:T(8,128)}, f32[128,512]{1,0:T(8,128)S(1)}, u32[]{:S(2)}, u32[]{:S(2)}) collective-permute-start(f32[128,512]{1,0:T(8,128)} %add.735), channel_id=1, source_target_pairs={{15,0},{0,1},{1,2},{2,3},{3,4},{4,5},{5,6},{6,7},{7,8},{8,9},{9,10... | collective-permute-start | bytes 786440 | tf_op jit(solution)/shard_map/while/body/eval_jaxpr/ppermute | solution.py:17
  677.2 18.3 %conditional.12 = (f32[2048,512]{1,0:T(8,128)}, f32[2048,64]{0,1:T(8,128)}, f32[128,512]{1,0:T(8,128)}, f32[128,64]{0,1:T(8,128)}) conditional(s32[]{:T(128)} %clamp.53, (f32[2048,512]{1,0:T(8,128)}, f32[2048,64]{0,1:T(8,128)}) %tuple.143, (pred[]{:T(512)}, s32[128]{0:T(128)S(1)}, s32[64,32]{1,0:T(8,128)}, ...), branch_computations={%region_4.4_spmd, %region_5.5_spmd, %region_6.6_spmd} | conditional | flops 1446969344 | bytes 44311128 | solution.py:114
  698.5 23.0 %collective-permute-start.4 = (f32[128,512]{1,0:T(8,128)}, f32[128,512]{1,0:T(8,128)}, u32[]{:S(2)}, u32[]{:S(2)}) collective-permute-start(f32[128,512]{1,0:T(8,128)} %add.732), channel_id=1, source_target_pairs={{15,0},{0,1},{1,2},{2,3},{3,4},{4,5},{5,6},{6,7},{7,8},{8,9},{9,10... | collective-permute-start | bytes 786440 | tf_op jit(solution)/shard_map/while/body/eval_jaxpr/ppermute | solution.py:17
  727.9 17.9 %conditional.14 = (f32[2048,512]{1,0:T(8,128)}, f32[2048,64]{0,1:T(8,128)}, f32[128,512]{1,0:T(8,128)}, f32[128,64]{0,1:T(8,128)}) conditional(s32[]{:T(128)} %clamp.55, (f32[2048,512]{1,0:T(8,128)}, f32[2048,64]{0,1:T(8,128)}) %tuple.149, (pred[]{:T(512)}, s32[128]{0:T(128)S(1)}, s32[64,32]{1,0:T(8,128)}, ...), branch_computations={%region_11.11_spmd, %region_12.12_spmd, %region_13.13_spmd} | conditional | flops 1446969344 | bytes 44311128 | solution.py:114
  747.6 16.9 %collective-permute-start.5 = (f32[128,512]{1,0:T(8,128)}, f32[128,512]{1,0:T(8,128)S(1)}, u32[]{:S(2)}, u32[]{:S(2)}) collective-permute-start(f32[128,512]{1,0:T(8,128)} %add.735), channel_id=1, source_target_pairs={{15,0},{0,1},{1,2},{2,3},{3,4},{4,5},{5,6},{6,7},{7,8},{8,9},{9,10... | collective-permute-start | bytes 786440 | tf_op jit(solution)/shard_map/while/body/eval_jaxpr/ppermute | solution.py:17
  765.2 6.7 collective-permute-done.6
  791.0 18.3 %conditional.12 = (f32[2048,512]{1,0:T(8,128)}, f32[2048,64]{0,1:T(8,128)}, f32[128,512]{1,0:T(8,128)}, f32[128,64]{0,1:T(8,128)}) conditional(s32[]{:T(128)} %clamp.53, (f32[2048,512]{1,0:T(8,128)}, f32[2048,64]{0,1:T(8,128)}) %tuple.143, (pred[]{:T(512)}, s32[128]{0:T(128)S(1)}, s32[64,32]{1,0:T(8,128)}, ...), branch_computations={%region_4.4_spmd, %region_5.5_spmd, %region_6.6_spmd} | conditional | flops 1446969344 | bytes 44311128 | solution.py:114
  812.4 21.3 %collective-permute-start.4 = (f32[128,512]{1,0:T(8,128)}, f32[128,512]{1,0:T(8,128)}, u32[]{:S(2)}, u32[]{:S(2)}) collective-permute-start(f32[128,512]{1,0:T(8,128)} %add.732), channel_id=1, source_target_pairs={{15,0},{0,1},{1,2},{2,3},{3,4},{4,5},{5,6},{6,7},{7,8},{8,9},{9,10... | collective-permute-start | bytes 786440 | tf_op jit(solution)/shard_map/while/body/eval_jaxpr/ppermute | solution.py:17
  840.0 19.0 %conditional.14 = (f32[2048,512]{1,0:T(8,128)}, f32[2048,64]{0,1:T(8,128)}, f32[128,512]{1,0:T(8,128)}, f32[128,64]{0,1:T(8,128)}) conditional(s32[]{:T(128)} %clamp.55, (f32[2048,512]{1,0:T(8,128)}, f32[2048,64]{0,1:T(8,128)}) %tuple.149, (pred[]{:T(512)}, s32[128]{0:T(128)S(1)}, s32[64,32]{1,0:T(8,128)}, ...), branch_computations={%region_11.11_spmd, %region_12.12_spmd, %region_13.13_spmd} | conditional | flops 1446969344 | bytes 44311128 | solution.py:114
  859.0 15.7 %conditional.15 = ((f32[2048,512]{1,0:T(8,128)}, f32[2048,64]{0,1:T(8,128)}, f32[128,512]{1,0:T(8,128)}, f32[128,64]{0,1:T(8,128)})) conditional(s32[]{:T(128)} %clamp.54, (f32[2048,512]{1,0:T(8,128)}, f32[2048,64]{0,1:T(8,128)}, f32[128,512]{1,0:T(8,128)}, f32[128,64]{0,1:T(8,128)}) %tuple.152, (pred[]{:T(512)}, ...), branch_computations={%region_14.14_spmd, %region_15.15_spmd, %region_16.16_spmd} | conditional | flops 1447043072 | bytes 36217412 | solution.py:114
  877.3 9.7 collective-permute-done.6
  906.8 18.3 %conditional.12 = (f32[2048,512]{1,0:T(8,128)}, f32[2048,64]{0,1:T(8,128)}, f32[128,512]{1,0:T(8,128)}, f32[128,64]{0,1:T(8,128)}) conditional(s32[]{:T(128)} %clamp.53, (f32[2048,512]{1,0:T(8,128)}, f32[2048,64]{0,1:T(8,128)}) %tuple.143, (pred[]{:T(512)}, s32[128]{0:T(128)S(1)}, s32[64,32]{1,0:T(8,128)}, ...), branch_computations={%region_4.4_spmd, %region_5.5_spmd, %region_6.6_spmd} | conditional | flops 1446969344 | bytes 44311128 | solution.py:114
  928.2 22.3 %collective-permute-start.4 = (f32[128,512]{1,0:T(8,128)}, f32[128,512]{1,0:T(8,128)}, u32[]{:S(2)}, u32[]{:S(2)}) collective-permute-start(f32[128,512]{1,0:T(8,128)} %add.732), channel_id=1, source_target_pairs={{15,0},{0,1},{1,2},{2,3},{3,4},{4,5},{5,6},{6,7},{7,8},{8,9},{9,10... | collective-permute-start | bytes 786440 | tf_op jit(solution)/shard_map/while/body/eval_jaxpr/ppermute | solution.py:17
  956.9 17.9 %conditional.14 = (f32[2048,512]{1,0:T(8,128)}, f32[2048,64]{0,1:T(8,128)}, f32[128,512]{1,0:T(8,128)}, f32[128,64]{0,1:T(8,128)}) conditional(s32[]{:T(128)} %clamp.55, (f32[2048,512]{1,0:T(8,128)}, f32[2048,64]{0,1:T(8,128)}) %tuple.149, (pred[]{:T(512)}, s32[128]{0:T(128)S(1)}, s32[64,32]{1,0:T(8,128)}, ...), branch_computations={%region_11.11_spmd, %region_12.12_spmd, %region_13.13_spmd} | conditional | flops 1446969344 | bytes 44311128 | solution.py:114
  976.5 16.7 %collective-permute-start.5 = (f32[128,512]{1,0:T(8,128)}, f32[128,512]{1,0:T(8,128)S(1)}, u32[]{:S(2)}, u32[]{:S(2)}) collective-permute-start(f32[128,512]{1,0:T(8,128)} %add.735), channel_id=1, source_target_pairs={{15,0},{0,1},{1,2},{2,3},{3,4},{4,5},{5,6},{6,7},{7,8},{8,9},{9,10... | collective-permute-start | bytes 786440 | tf_op jit(solution)/shard_map/while/body/eval_jaxpr/ppermute | solution.py:17
  994.0 6.7 collective-permute-done.6
  1015.8 8.4 fusion.129
  1024.3 9.0 copy.98
  1037.6 7.1 fusion.135
  1046.0 12.6 %all-reduce.2 = (bf16[128,512]{1,0:T(8,128)(2,1)}, bf16[128,64]{0,1:T(8,128)(2,1)}) all-reduce(f32[128,512]{1,0:T(8,128)S(1)} %copy-done.17, f32[128,64]{0,1:T(8,128)} %get-tuple-element.1040), channel_id=1, replica_groups=mesh['head'=2,'inner'=2,'outer'=8] {'head'}, use_global_device_ids=true, to_apply=%region_18.19 | all-reduce | flops 73728 | bytes 442368 | tf_op jit(solution)/shard_map/psum | solution.py:201
  1058.7 77.5 %reduce-scatter.3.cloned.1.call-done = f32[32,4096]{1,0:T(8,128)} async-done(((f32[512,4096]{1,0:T(8,128)}), f32[32,4096]{1,0:T(8,128)}) %reduce-scatter.3.cloned.1.call-update) | async-done | bytes 524304 | tf_op jit(solution)/shard_map/reduce_scatter | solution.py:215
  (689 shorter events, 630.9 us)
Async XLA Ops:
  7.2 1051.5 %reduce-scatter.5.cloned.1.call-start = ((), (), s32[]{:S(2)}) async-start(), calls=%async_computation.3 | async-start | bytes 8912896 | tf_op jit(solution)/shard_map/reduce_scatter | solution.py:221
  32.9 1103.3 %reduce-scatter.3.cloned.1.call-start = ((), (), s32[]{:S(2)}) async-start(), calls=%async_computation.2 | async-start | bytes 8912896 | tf_op jit(solution)/shard_map/reduce_scatter | solution.py:215
  98.3 60.3 %collective-permute-start.2 = (bf16[128,64]{1,0:T(8,128)(2,1)}, bf16[128,64]{1,0:T(8,128)(2,1)}, u32[]{:S(2)}, u32[]{:S(2)}) collective-permute-start(bf16[128,64]{1,0:T(8,128)(2,1)} %get-tuple-element.1591), channel_id=1, source_target_pairs={{15,0},{0,1},{1,2},{2,3},{3,4},{4,5},{5,6},{6,7},{7,8},{8,9},{9,10... | collective-permute-start | bytes 49160 | tf_op jit(solution)/shard_map/while/body/eval_jaxpr/ppermute | solution.py:17
  98.7 59.9 %collective-permute-start = (bf16[128,512]{1,0:T(8,128)(2,1)}, bf16[128,512]{1,0:T(8,128)(2,1)S(1)}, u32[]{:S(2)}, u32[]{:S(2)}) collective-permute-start(bf16[128,512]{1,0:T(8,128)(2,1)} %get-tuple-element.1590), channel_id=1, source_target_pairs={{15,0},{0,1},{1,2},{2,3},{3,4},{4,5},{5,6},{6,7},{7,8},{8,9},{9,10... | collective-permute-start | bytes 393224 | tf_op jit(solution)/shard_map/while/body/eval_jaxpr/ppermute | solution.py:17
  152.3 41.1 %collective-permute-start.4 = (f32[128,512]{1,0:T(8,128)}, f32[128,512]{1,0:T(8,128)}, u32[]{:S(2)}, u32[]{:S(2)}) collective-permute-start(f32[128,512]{1,0:T(8,128)} %add.732), channel_id=1, source_target_pairs={{15,0},{0,1},{1,2},{2,3},{3,4},{4,5},{5,6},{6,7},{7,8},{8,9},{9,10... | collective-permute-start | bytes 786440 | tf_op jit(solution)/shard_map/while/body/eval_jaxpr/ppermute | solution.py:17
  195.2 18.5 %collective-permute-start.5 = (f32[128,512]{1,0:T(8,128)}, f32[128,512]{1,0:T(8,128)S(1)}, u32[]{:S(2)}, u32[]{:S(2)}) collective-permute-start(f32[128,512]{1,0:T(8,128)} %add.735), channel_id=1, source_target_pairs={{15,0},{0,1},{1,2},{2,3},{3,4},{4,5},{5,6},{6,7},{7,8},{8,9},{9,10... | collective-permute-start | bytes 786440 | tf_op jit(solution)/shard_map/while/body/eval_jaxpr/ppermute | solution.py:17
  198.1 15.6 %collective-permute-start.1 = (bf16[128,512]{1,0:T(8,128)(2,1)S(1)}, bf16[128,512]{1,0:T(8,128)(2,1)}, u32[]{:S(2)}, u32[]{:S(2)}) collective-permute-start(bf16[128,512]{1,0:T(8,128)(2,1)S(1)} %collective-permute-done), channel_id=1, source_target_pairs={{15,0},{0,1},{1,2},{2,3},{3,4},{4,5},{5,6},{6,7},{7,8},{8,9},{9,10... | collective-permute-start | bytes 393224 | tf_op jit(solution)/shard_map/while/body/eval_jaxpr/ppermute | solution.py:17
  214.4 57.5 %collective-permute-start.2 = (bf16[128,64]{1,0:T(8,128)(2,1)}, bf16[128,64]{1,0:T(8,128)(2,1)}, u32[]{:S(2)}, u32[]{:S(2)}) collective-permute-start(bf16[128,64]{1,0:T(8,128)(2,1)} %get-tuple-element.1591), channel_id=1, source_target_pairs={{15,0},{0,1},{1,2},{2,3},{3,4},{4,5},{5,6},{6,7},{7,8},{8,9},{9,10... | collective-permute-start | bytes 49160 | tf_op jit(solution)/shard_map/while/body/eval_jaxpr/ppermute | solution.py:17
  214.4 57.5 %collective-permute-start = (bf16[128,512]{1,0:T(8,128)(2,1)}, bf16[128,512]{1,0:T(8,128)(2,1)S(1)}, u32[]{:S(2)}, u32[]{:S(2)}) collective-permute-start(bf16[128,512]{1,0:T(8,128)(2,1)} %get-tuple-element.1590), channel_id=1, source_target_pairs={{15,0},{0,1},{1,2},{2,3},{3,4},{4,5},{5,6},{6,7},{7,8},{8,9},{9,10... | collective-permute-start | bytes 393224 | tf_op jit(solution)/shard_map/while/body/eval_jaxpr/ppermute | solution.py:17
  246.1 60.5 %collective-permute-start.4 = (f32[128,512]{1,0:T(8,128)}, f32[128,512]{1,0:T(8,128)}, u32[]{:S(2)}, u32[]{:S(2)}) collective-permute-start(f32[128,512]{1,0:T(8,128)} %add.732), channel_id=1, source_target_pairs={{15,0},{0,1},{1,2},{2,3},{3,4},{4,5},{5,6},{6,7},{7,8},{8,9},{9,10... | collective-permute-start | bytes 786440 | tf_op jit(solution)/shard_map/while/body/eval_jaxpr/ppermute | solution.py:17
  308.3 18.5 %collective-permute-start.5 = (f32[128,512]{1,0:T(8,128)}, f32[128,512]{1,0:T(8,128)S(1)}, u32[]{:S(2)}, u32[]{:S(2)}) collective-permute-start(f32[128,512]{1,0:T(8,128)} %add.735), channel_id=1, source_target_pairs={{15,0},{0,1},{1,2},{2,3},{3,4},{4,5},{5,6},{6,7},{7,8},{8,9},{9,10... | collective-permute-start | bytes 786440 | tf_op jit(solution)/shard_map/while/body/eval_jaxpr/ppermute | solution.py:17
  310.2 16.7 %collective-permute-start.1 = (bf16[128,512]{1,0:T(8,128)(2,1)S(1)}, bf16[128,512]{1,0:T(8,128)(2,1)}, u32[]{:S(2)}, u32[]{:S(2)}) collective-permute-start(bf16[128,512]{1,0:T(8,128)(2,1)S(1)} %collective-permute-done), channel_id=1, source_target_pairs={{15,0},{0,1},{1,2},{2,3},{3,4},{4,5},{5,6},{6,7},{7,8},{8,9},{9,10... | collective-permute-start | bytes 393224 | tf_op jit(solution)/shard_map/while/body/eval_jaxpr/ppermute | solution.py:17
  311.0 7.8 collective-permute-start.6
  320.2 6.7 collective-permute-start.7
  327.6 59.1 %collective-permute-start.2 = (bf16[128,64]{1,0:T(8,128)(2,1)}, bf16[128,64]{1,0:T(8,128)(2,1)}, u32[]{:S(2)}, u32[]{:S(2)}) collective-permute-start(bf16[128,64]{1,0:T(8,128)(2,1)} %get-tuple-element.1591), channel_id=1, source_target_pairs={{15,0},{0,1},{1,2},{2,3},{3,4},{4,5},{5,6},{6,7},{7,8},{8,9},{9,10... | collective-permute-start | bytes 49160 | tf_op jit(solution)/shard_map/while/body/eval_jaxpr/ppermute | solution.py:17
  327.6 59.1 %collective-permute-start = (bf16[128,512]{1,0:T(8,128)(2,1)}, bf16[128,512]{1,0:T(8,128)(2,1)S(1)}, u32[]{:S(2)}, u32[]{:S(2)}) collective-permute-start(bf16[128,512]{1,0:T(8,128)(2,1)} %get-tuple-element.1590), channel_id=1, source_target_pairs={{15,0},{0,1},{1,2},{2,3},{3,4},{4,5},{5,6},{6,7},{7,8},{8,9},{9,10... | collective-permute-start | bytes 393224 | tf_op jit(solution)/shard_map/while/body/eval_jaxpr/ppermute | solution.py:17
  359.3 45.3 %collective-permute-start.4 = (f32[128,512]{1,0:T(8,128)}, f32[128,512]{1,0:T(8,128)}, u32[]{:S(2)}, u32[]{:S(2)}) collective-permute-start(f32[128,512]{1,0:T(8,128)} %add.732), channel_id=1, source_target_pairs={{15,0},{0,1},{1,2},{2,3},{3,4},{4,5},{5,6},{6,7},{7,8},{8,9},{9,10... | collective-permute-start | bytes 786440 | tf_op jit(solution)/shard_map/while/body/eval_jaxpr/ppermute | solution.py:17
  406.4 34.1 %collective-permute-start.5 = (f32[128,512]{1,0:T(8,128)}, f32[128,512]{1,0:T(8,128)S(1)}, u32[]{:S(2)}, u32[]{:S(2)}) collective-permute-start(f32[128,512]{1,0:T(8,128)} %add.735), channel_id=1, source_target_pairs={{15,0},{0,1},{1,2},{2,3},{3,4},{4,5},{5,6},{6,7},{7,8},{8,9},{9,10... | collective-permute-start | bytes 786440 | tf_op jit(solution)/shard_map/while/body/eval_jaxpr/ppermute | solution.py:17
  408.9 31.6 %collective-permute-start.1 = (bf16[128,512]{1,0:T(8,128)(2,1)S(1)}, bf16[128,512]{1,0:T(8,128)(2,1)}, u32[]{:S(2)}, u32[]{:S(2)}) collective-permute-start(bf16[128,512]{1,0:T(8,128)(2,1)S(1)} %collective-permute-done), channel_id=1, source_target_pairs={{15,0},{0,1},{1,2},{2,3},{3,4},{4,5},{5,6},{6,7},{7,8},{8,9},{9,10... | collective-permute-start | bytes 393224 | tf_op jit(solution)/shard_map/while/body/eval_jaxpr/ppermute | solution.py:17
  441.3 38.0 %collective-permute-start.2 = (bf16[128,64]{1,0:T(8,128)(2,1)}, bf16[128,64]{1,0:T(8,128)(2,1)}, u32[]{:S(2)}, u32[]{:S(2)}) collective-permute-start(bf16[128,64]{1,0:T(8,128)(2,1)} %get-tuple-element.1591), channel_id=1, source_target_pairs={{15,0},{0,1},{1,2},{2,3},{3,4},{4,5},{5,6},{6,7},{7,8},{8,9},{9,10... | collective-permute-start | bytes 49160 | tf_op jit(solution)/shard_map/while/body/eval_jaxpr/ppermute | solution.py:17
  441.3 38.0 %collective-permute-start = (bf16[128,512]{1,0:T(8,128)(2,1)}, bf16[128,512]{1,0:T(8,128)(2,1)S(1)}, u32[]{:S(2)}, u32[]{:S(2)}) collective-permute-start(bf16[128,512]{1,0:T(8,128)(2,1)} %get-tuple-element.1590), channel_id=1, source_target_pairs={{15,0},{0,1},{1,2},{2,3},{3,4},{4,5},{5,6},{6,7},{7,8},{8,9},{9,10... | collective-permute-start | bytes 393224 | tf_op jit(solution)/shard_map/while/body/eval_jaxpr/ppermute | solution.py:17
  472.9 41.0 %collective-permute-start.4 = (f32[128,512]{1,0:T(8,128)}, f32[128,512]{1,0:T(8,128)}, u32[]{:S(2)}, u32[]{:S(2)}) collective-permute-start(f32[128,512]{1,0:T(8,128)} %add.732), channel_id=1, source_target_pairs={{15,0},{0,1},{1,2},{2,3},{3,4},{4,5},{5,6},{6,7},{7,8},{8,9},{9,10... | collective-permute-start | bytes 786440 | tf_op jit(solution)/shard_map/while/body/eval_jaxpr/ppermute | solution.py:17
  515.7 32.6 %collective-permute-start.5 = (f32[128,512]{1,0:T(8,128)}, f32[128,512]{1,0:T(8,128)S(1)}, u32[]{:S(2)}, u32[]{:S(2)}) collective-permute-start(f32[128,512]{1,0:T(8,128)} %add.735), channel_id=1, source_target_pairs={{15,0},{0,1},{1,2},{2,3},{3,4},{4,5},{5,6},{6,7},{7,8},{8,9},{9,10... | collective-permute-start | bytes 786440 | tf_op jit(solution)/shard_map/while/body/eval_jaxpr/ppermute | solution.py:17
  515.7 32.6 %collective-permute-start.1 = (bf16[128,512]{1,0:T(8,128)(2,1)S(1)}, bf16[128,512]{1,0:T(8,128)(2,1)}, u32[]{:S(2)}, u32[]{:S(2)}) collective-permute-start(bf16[128,512]{1,0:T(8,128)(2,1)S(1)} %collective-permute-done), channel_id=1, source_target_pairs={{15,0},{0,1},{1,2},{2,3},{3,4},{4,5},{5,6},{6,7},{7,8},{8,9},{9,10... | collective-permute-start | bytes 393224 | tf_op jit(solution)/shard_map/while/body/eval_jaxpr/ppermute | solution.py:17
  516.5 9.7 collective-permute-start.6
  527.5 20.7 %collective-permute-start.7 = (f32[128,64]{0,1:T(8,128)}, f32[128,64]{0,1:T(8,128)}, u32[]{:S(2)}, u32[]{:S(2)}) collective-permute-start(f32[128,64]{0,1:T(8,128)} %add.737), channel_id=1, source_target_pairs={{15,0},{0,1},{1,2},{2,3},{3,4},{4,5},{5,6},{6,7},{7,8},{8,9},{9,10... | collective-permute-start | bytes 98312 | tf_op jit(solution)/shard_map/while/body/eval_jaxpr/ppermute | solution.py:17
  549.0 63.3 %collective-permute-start.2 = (bf16[128,64]{1,0:T(8,128)(2,1)}, bf16[128,64]{1,0:T(8,128)(2,1)}, u32[]{:S(2)}, u32[]{:S(2)}) collective-permute-start(bf16[128,64]{1,0:T(8,128)(2,1)} %get-tuple-element.1591), channel_id=1, source_target_pairs={{15,0},{0,1},{1,2},{2,3},{3,4},{4,5},{5,6},{6,7},{7,8},{8,9},{9,10... | collective-permute-start | bytes 49160 | tf_op jit(solution)/shard_map/while/body/eval_jaxpr/ppermute | solution.py:17
  549.6 62.7 %collective-permute-start = (bf16[128,512]{1,0:T(8,128)(2,1)}, bf16[128,512]{1,0:T(8,128)(2,1)S(1)}, u32[]{:S(2)}, u32[]{:S(2)}) collective-permute-start(bf16[128,512]{1,0:T(8,128)(2,1)} %get-tuple-element.1590), channel_id=1, source_target_pairs={{15,0},{0,1},{1,2},{2,3},{3,4},{4,5},{5,6},{6,7},{7,8},{8,9},{9,10... | collective-permute-start | bytes 393224 | tf_op jit(solution)/shard_map/while/body/eval_jaxpr/ppermute | solution.py:17
  583.6 46.6 %collective-permute-start.4 = (f32[128,512]{1,0:T(8,128)}, f32[128,512]{1,0:T(8,128)}, u32[]{:S(2)}, u32[]{:S(2)}) collective-permute-start(f32[128,512]{1,0:T(8,128)} %add.732), channel_id=1, source_target_pairs={{15,0},{0,1},{1,2},{2,3},{3,4},{4,5},{5,6},{6,7},{7,8},{8,9},{9,10... | collective-permute-start | bytes 786440 | tf_op jit(solution)/shard_map/while/body/eval_jaxpr/ppermute | solution.py:17
  632.0 32.3 %collective-permute-start.5 = (f32[128,512]{1,0:T(8,128)}, f32[128,512]{1,0:T(8,128)S(1)}, u32[]{:S(2)}, u32[]{:S(2)}) collective-permute-start(f32[128,512]{1,0:T(8,128)} %add.735), channel_id=1, source_target_pairs={{15,0},{0,1},{1,2},{2,3},{3,4},{4,5},{5,6},{6,7},{7,8},{8,9},{9,10... | collective-permute-start | bytes 786440 | tf_op jit(solution)/shard_map/while/body/eval_jaxpr/ppermute | solution.py:17
  648.7 15.5 %collective-permute-start.1 = (bf16[128,512]{1,0:T(8,128)(2,1)S(1)}, bf16[128,512]{1,0:T(8,128)(2,1)}, u32[]{:S(2)}, u32[]{:S(2)}) collective-permute-start(bf16[128,512]{1,0:T(8,128)(2,1)S(1)} %collective-permute-done), channel_id=1, source_target_pairs={{15,0},{0,1},{1,2},{2,3},{3,4},{4,5},{5,6},{6,7},{7,8},{8,9},{9,10... | collective-permute-start | bytes 393224 | tf_op jit(solution)/shard_map/while/body/eval_jaxpr/ppermute | solution.py:17
  665.0 62.9 %collective-permute-start.2 = (bf16[128,64]{1,0:T(8,128)(2,1)}, bf16[128,64]{1,0:T(8,128)(2,1)}, u32[]{:S(2)}, u32[]{:S(2)}) collective-permute-start(bf16[128,64]{1,0:T(8,128)(2,1)} %get-tuple-element.1591), channel_id=1, source_target_pairs={{15,0},{0,1},{1,2},{2,3},{3,4},{4,5},{5,6},{6,7},{7,8},{8,9},{9,10... | collective-permute-start | bytes 49160 | tf_op jit(solution)/shard_map/while/body/eval_jaxpr/ppermute | solution.py:17
  665.0 62.9 %collective-permute-start = (bf16[128,512]{1,0:T(8,128)(2,1)}, bf16[128,512]{1,0:T(8,128)(2,1)S(1)}, u32[]{:S(2)}, u32[]{:S(2)}) collective-permute-start(bf16[128,512]{1,0:T(8,128)(2,1)} %get-tuple-element.1590), channel_id=1, source_target_pairs={{15,0},{0,1},{1,2},{2,3},{3,4},{4,5},{5,6},{6,7},{7,8},{8,9},{9,10... | collective-permute-start | bytes 393224 | tf_op jit(solution)/shard_map/while/body/eval_jaxpr/ppermute | solution.py:17
  698.5 47.3 %collective-permute-start.4 = (f32[128,512]{1,0:T(8,128)}, f32[128,512]{1,0:T(8,128)}, u32[]{:S(2)}, u32[]{:S(2)}) collective-permute-start(f32[128,512]{1,0:T(8,128)} %add.732), channel_id=1, source_target_pairs={{15,0},{0,1},{1,2},{2,3},{3,4},{4,5},{5,6},{6,7},{7,8},{8,9},{9,10... | collective-permute-start | bytes 786440 | tf_op jit(solution)/shard_map/while/body/eval_jaxpr/ppermute | solution.py:17
  747.6 32.4 %collective-permute-start.5 = (f32[128,512]{1,0:T(8,128)}, f32[128,512]{1,0:T(8,128)S(1)}, u32[]{:S(2)}, u32[]{:S(2)}) collective-permute-start(f32[128,512]{1,0:T(8,128)} %add.735), channel_id=1, source_target_pairs={{15,0},{0,1},{1,2},{2,3},{3,4},{4,5},{5,6},{6,7},{7,8},{8,9},{9,10... | collective-permute-start | bytes 786440 | tf_op jit(solution)/shard_map/while/body/eval_jaxpr/ppermute | solution.py:17
  764.4 15.5 %collective-permute-start.1 = (bf16[128,512]{1,0:T(8,128)(2,1)S(1)}, bf16[128,512]{1,0:T(8,128)(2,1)}, u32[]{:S(2)}, u32[]{:S(2)}) collective-permute-start(bf16[128,512]{1,0:T(8,128)(2,1)S(1)} %collective-permute-done), channel_id=1, source_target_pairs={{15,0},{0,1},{1,2},{2,3},{3,4},{4,5},{5,6},{6,7},{7,8},{8,9},{9,10... | collective-permute-start | bytes 393224 | tf_op jit(solution)/shard_map/while/body/eval_jaxpr/ppermute | solution.py:17
  780.7 59.3 %collective-permute-start.2 = (bf16[128,64]{1,0:T(8,128)(2,1)}, bf16[128,64]{1,0:T(8,128)(2,1)}, u32[]{:S(2)}, u32[]{:S(2)}) collective-permute-start(bf16[128,64]{1,0:T(8,128)(2,1)} %get-tuple-element.1591), channel_id=1, source_target_pairs={{15,0},{0,1},{1,2},{2,3},{3,4},{4,5},{5,6},{6,7},{7,8},{8,9},{9,10... | collective-permute-start | bytes 49160 | tf_op jit(solution)/shard_map/while/body/eval_jaxpr/ppermute | solution.py:17
  780.7 59.3 %collective-permute-start = (bf16[128,512]{1,0:T(8,128)(2,1)}, bf16[128,512]{1,0:T(8,128)(2,1)S(1)}, u32[]{:S(2)}, u32[]{:S(2)}) collective-permute-start(bf16[128,512]{1,0:T(8,128)(2,1)} %get-tuple-element.1590), channel_id=1, source_target_pairs={{15,0},{0,1},{1,2},{2,3},{3,4},{4,5},{5,6},{6,7},{7,8},{8,9},{9,10... | collective-permute-start | bytes 393224 | tf_op jit(solution)/shard_map/while/body/eval_jaxpr/ppermute | solution.py:17
  812.4 62.3 %collective-permute-start.4 = (f32[128,512]{1,0:T(8,128)}, f32[128,512]{1,0:T(8,128)}, u32[]{:S(2)}, u32[]{:S(2)}) collective-permute-start(f32[128,512]{1,0:T(8,128)} %add.732), channel_id=1, source_target_pairs={{15,0},{0,1},{1,2},{2,3},{3,4},{4,5},{5,6},{6,7},{7,8},{8,9},{9,10... | collective-permute-start | bytes 786440 | tf_op jit(solution)/shard_map/while/body/eval_jaxpr/ppermute | solution.py:17
  876.5 18.5 %collective-permute-start.5 = (f32[128,512]{1,0:T(8,128)}, f32[128,512]{1,0:T(8,128)S(1)}, u32[]{:S(2)}, u32[]{:S(2)}) collective-permute-start(f32[128,512]{1,0:T(8,128)} %add.735), channel_id=1, source_target_pairs={{15,0},{0,1},{1,2},{2,3},{3,4},{4,5},{5,6},{6,7},{7,8},{8,9},{9,10... | collective-permute-start | bytes 786440 | tf_op jit(solution)/shard_map/while/body/eval_jaxpr/ppermute | solution.py:17
  876.5 18.5 %collective-permute-start.1 = (bf16[128,512]{1,0:T(8,128)(2,1)S(1)}, bf16[128,512]{1,0:T(8,128)(2,1)}, u32[]{:S(2)}, u32[]{:S(2)}) collective-permute-start(bf16[128,512]{1,0:T(8,128)(2,1)S(1)} %collective-permute-done), channel_id=1, source_target_pairs={{15,0},{0,1},{1,2},{2,3},{3,4},{4,5},{5,6},{6,7},{7,8},{8,9},{9,10... | collective-permute-start | bytes 393224 | tf_op jit(solution)/shard_map/while/body/eval_jaxpr/ppermute | solution.py:17
  877.2 9.7 collective-permute-start.6
  895.7 61.1 %collective-permute-start.2 = (bf16[128,64]{1,0:T(8,128)(2,1)}, bf16[128,64]{1,0:T(8,128)(2,1)}, u32[]{:S(2)}, u32[]{:S(2)}) collective-permute-start(bf16[128,64]{1,0:T(8,128)(2,1)} %get-tuple-element.1591), channel_id=1, source_target_pairs={{15,0},{0,1},{1,2},{2,3},{3,4},{4,5},{5,6},{6,7},{7,8},{8,9},{9,10... | collective-permute-start | bytes 49160 | tf_op jit(solution)/shard_map/while/body/eval_jaxpr/ppermute | solution.py:17
  895.7 61.1 %collective-permute-start = (bf16[128,512]{1,0:T(8,128)(2,1)}, bf16[128,512]{1,0:T(8,128)(2,1)S(1)}, u32[]{:S(2)}, u32[]{:S(2)}) collective-permute-start(bf16[128,512]{1,0:T(8,128)(2,1)} %get-tuple-element.1590), channel_id=1, source_target_pairs={{15,0},{0,1},{1,2},{2,3},{3,4},{4,5},{5,6},{6,7},{7,8},{8,9},{9,10... | collective-permute-start | bytes 393224 | tf_op jit(solution)/shard_map/while/body/eval_jaxpr/ppermute | solution.py:17
  928.2 46.5 %collective-permute-start.4 = (f32[128,512]{1,0:T(8,128)}, f32[128,512]{1,0:T(8,128)}, u32[]{:S(2)}, u32[]{:S(2)}) collective-permute-start(f32[128,512]{1,0:T(8,128)} %add.732), channel_id=1, source_target_pairs={{15,0},{0,1},{1,2},{2,3},{3,4},{4,5},{5,6},{6,7},{7,8},{8,9},{9,10... | collective-permute-start | bytes 786440 | tf_op jit(solution)/shard_map/while/body/eval_jaxpr/ppermute | solution.py:17
  976.5 32.3 %collective-permute-start.5 = (f32[128,512]{1,0:T(8,128)}, f32[128,512]{1,0:T(8,128)S(1)}, u32[]{:S(2)}, u32[]{:S(2)}) collective-permute-start(f32[128,512]{1,0:T(8,128)} %add.735), channel_id=1, source_target_pairs={{15,0},{0,1},{1,2},{2,3},{3,4},{4,5},{5,6},{6,7},{7,8},{8,9},{9,10... | collective-permute-start | bytes 786440 | tf_op jit(solution)/shard_map/while/body/eval_jaxpr/ppermute | solution.py:17
  993.2 15.5 %collective-permute-start.1 = (bf16[128,512]{1,0:T(8,128)(2,1)S(1)}, bf16[128,512]{1,0:T(8,128)(2,1)}, u32[]{:S(2)}, u32[]{:S(2)}) collective-permute-start(bf16[128,512]{1,0:T(8,128)(2,1)S(1)} %collective-permute-done), channel_id=1, source_target_pairs={{15,0},{0,1},{1,2},{2,3},{3,4},{4,5},{5,6},{6,7},{7,8},{8,9},{9,10... | collective-permute-start | bytes 393224 | tf_op jit(solution)/shard_map/while/body/eval_jaxpr/ppermute | solution.py:17
  1002.0 6.7 collective-permute-start.7
  (92 other events, 570.7 us)
Sparse Core Ops, SparseCore 0:
  33.0 107.4 reduce-scatter.4
  1033.4 102.7 reduce-scatter.2
where the time goes:
time: 1160 us; the launch traced here: 1140 us
  matrix products  333 us (29%)
  starting transfers between devices  243 us (21%)
  local copies, waits for them, and re-layouts  197 us (17%)
  waiting for transfers between devices  175 us (15%)
  loops' own time  98.5 us (8%)
  other arithmetic  69.9 us (6%)
  between operations  14.7 us (1%)
  blocking collectives  12.6 us (1%)
    ppermute x64, starting transfers between devices, shifted(): return lax.ppermute(block, axis, route)  243 us
    dot_general x42, matrix products, contract_first(): lax.dot_general(first_op, second_op, (((0,), (0,)), ((), ())), preferred_...  150 us
    another operation x1, loops' own time, local(): lax.fori_loop(0, context_size // 2, step_pair, ((latent, key_rope), start...  97.2 us
    ppermute x64, waiting for transfers between devices, shifted(): return lax.ppermute(block, axis, route)  97 us
    dot_general x63, matrix products, contract_last(): lax.dot_general(first_op, second_op, (((1,), (1,)), ((), ())), preferred_...  96.8 us
    reduce_scatter x1, waiting for transfers between devices, local(): lax.psum_scatter(key_weight.reshape(LATENT, head_count * NOPE_DIM), ('inn...  77.5 us
    add x32, other arithmetic, step_pair(): key_sums = (key_sums[0] + contribution[0], key_sums[1] + contribution[1])  45.5 us
    dot_general x21, matrix products, grad_update(): jnp.dot(rounded, queries[3], preferred_element_type=jnp.float32)  24.3 us
  transfers between devices with their start and end apart: 66, of which 17 were waited for; matrix products, arithmetic and copies ran while one was open for 49% of the time, Pallas kernels for 0%

commit v1 on v0

v1 whole, which is shorter than its diff:
```python
import functools

import jax
import jax.numpy as jnp
from jax import lax
from jax.experimental import pallas as pl
from jax.experimental.pallas import tpu as pltpu
from jax.sharding import PartitionSpec as P

LATENT = 512
ROPE_DIM = 64
NOPE_DIM = 128
VALUE_DIM = 128
WIDE = 640
SPAN = 4
FACTOR = float(NOPE_DIM + ROPE_DIM) ** (-0.5)
VMEM = 60 * 1024 * 1024


def contract_last(first_op, second_op):
    return lax.dot_general(
        first_op, second_op, (((1,), (1,)), ((), ())), preferred_element_type=jnp.float32
    )


def contract_first(first_op, second_op):
    return lax.dot_general(
        first_op, second_op, (((0,), (0,)), ((), ())), preferred_element_type=jnp.float32
    )


def value_kernel(group, saved_ref, upstream_ref, out_ref):
    for h in range(group):
        saved = saved_ref[:, h * LATENT : (h + 1) * LATENT]
        upstream = upstream_ref[:, h * VALUE_DIM : (h + 1) * VALUE_DIM]
        out_ref[:, h * VALUE_DIM : (h + 1) * VALUE_DIM] = contract_first(saved, upstream).astype(
            out_ref.dtype
        )


def value_weights(latent_out, out_grad, group):
    tokens, width = out_grad.shape
    heads = width // VALUE_DIM
    return pl.pallas_call(
        functools.partial(value_kernel, group),
        grid=(heads // group,),
        in_specs=[
            pl.BlockSpec((tokens, group * LATENT), lambda i: (0, i)),
            pl.BlockSpec((tokens, group * VALUE_DIM), lambda i: (0, i)),
        ],
        out_specs=pl.BlockSpec((LATENT, group * VALUE_DIM), lambda i: (0, i)),
        out_shape=jax.ShapeDtypeStruct((LATENT, width), jnp.bfloat16),
        compiler_params=pltpu.CompilerParams(vmem_limit_bytes=VMEM),
        name="value_weights",
    )(latent_out, out_grad)


def attention_kernel(
    group,
    block,
    blocks,
    places_ref,
    nope_ref,
    rope_ref,
    lat_ref,
    key_rope_ref,
    key_up_ref,
    value_up_ref,
    saved_ref,
    upstream_ref,
    logsum_ref,
    d_nope_ref,
    d_rope_ref,
    d_keys_ref,
    key_weight_ref,
    keys,
    key_sums,
    queries,
    grads,
    delta,
    query_sums,
):
    rows = group * block
    tile = SPAN * block
    step = pl.program_id(0)

    @pl.when(step == 0)
    def _():
        def sort(p, carry):
            src = pl.ds(pl.multiple_of(places_ref[2 + p] * block, block), block)
            dst = pl.ds(pl.multiple_of(p * block, block), block)
            keys[dst, :LATENT] = lat_ref[src, :]
            part = key_rope_ref[src, :]
            keys[dst, LATENT:] = jnp.concatenate([part, jnp.zeros_like(part)], axis=1)
            return carry

        lax.fori_loop(0, blocks, sort, 0)
        key_sums[...] = jnp.zeros_like(key_sums)

    query_sums[...] = jnp.zeros_like(query_sums)
    for h in range(group):
        nope = nope_ref[:, h * NOPE_DIM : (h + 1) * NOPE_DIM]
        key_map = key_up_ref[:, h * NOPE_DIM : (h + 1) * NOPE_DIM]
        lat = contract_last(nope, key_map).astype(jnp.bfloat16)
        upstream = upstream_ref[:, h * VALUE_DIM : (h + 1) * VALUE_DIM]
        value_map = value_up_ref[:, h * VALUE_DIM : (h + 1) * VALUE_DIM]
        grad = contract_last(upstream, value_map).astype(jnp.bfloat16)
        for t in range(2):
            mine = slice(h * block, (h + 1) * block)
            held = slice(t * block, (t + 1) * block)
            queries[t, mine, :LATENT] = lat[held]
            part = rope_ref[held, h * ROPE_DIM : (h + 1) * ROPE_DIM]
            queries[t, mine, LATENT:] = jnp.concatenate([part, jnp.zeros_like(part)], axis=1)
            grads[t, mine, :] = grad[held]
    for t in range(2):
        held = slice(t * block, (t + 1) * block)
        for h in range(0, group, 2):
            saved = jnp.concatenate(
                [saved_ref[held, k * LATENT : (k + 1) * LATENT] for k in (h, h + 1)], axis=0
            )
            mine = slice(h * block, (h + 2) * block)
            product = grads[t, mine, :].astype(jnp.float32) * saved.astype(jnp.float32)
            folded = product[:, :128]
            for k in range(128, LATENT, 128):
                folded = folded + product[:, k : k + 128]
            delta[t, :, mine] = jnp.sum(folded.T, axis=0, keepdims=True)

    split = places_ref[0] // SPAN + 1
    key_index = lax.broadcasted_iota(jnp.int32, (tile, rows), 0)
    row_index = lax.rem(lax.broadcasted_iota(jnp.int32, (tile, rows), 1), block)
    apart = key_index - row_index

    def visit(i, carry):
        second = (i >= split).astype(jnp.int32)
        index = i - second * split
        place = places_ref[second]
        near = pl.ds(pl.multiple_of(index * tile, tile), tile)
        query = queries[second]
        grad = grads[second]
        held = keys[near, :]
        scores = contract_last(held, query) * FACTOR
        visible = apart <= place * block - index * tile
        weights = jnp.where(visible, jnp.exp(scores - logsum_ref[second]), 0.0)
        dprobs = contract_last(held[:, :LATENT], grad)
        dscore = (weights * (dprobs - delta[second]) * FACTOR).astype(jnp.bfloat16)
        rounded = weights.astype(jnp.bfloat16)
        query_sums[second] += contract_first(dscore, held)
        from_scores = jnp.dot(dscore, query, preferred_element_type=jnp.float32)
        from_values = jnp.dot(rounded, grad, preferred_element_type=jnp.float32)
        key_sums[near, :LATENT] += from_scores[:, :LATENT] + from_values
        key_sums[near, LATENT:] += from_scores[:, LATENT:]
        return carry

    lax.fori_loop(0, blocks // SPAN + 1, visit, 0)

    for h in range(group):
        mine = slice(h * block, (h + 1) * block)
        cols = slice(h * NOPE_DIM, (h + 1) * NOPE_DIM)
        grad_query = jnp.concatenate([query_sums[t, mine, :LATENT] for t in range(2)], axis=0)
        grad_query = grad_query.astype(jnp.bfloat16)
        key_map = key_up_ref[:, cols]
        d_nope_ref[:, cols] = jnp.dot(
            grad_query, key_map, preferred_element_type=jnp.float32
        ).astype(jnp.bfloat16)
        key_weight_ref[:, cols] = contract_first(grad_query, nope_ref[:, cols]).astype(
            key_weight_ref.dtype
        )
    for t in range(2):
        held = slice(t * block, (t + 1) * block)
        for h in range(0, group, 2):
            pair = [
                query_sums[t, k * block : (k + 1) * block, LATENT : LATENT + ROPE_DIM]
                for k in (h, h + 1)
            ]
            d_rope_ref[held, h * ROPE_DIM : (h + 2) * ROPE_DIM] = jnp.concatenate(
                pair, axis=1
            ).astype(jnp.bfloat16)

    @pl.when(step == pl.num_programs(0) - 1)
    def _():
        def restore(p, carry):
            dst = pl.ds(pl.multiple_of(places_ref[2 + p] * block, block), block)
            src = pl.ds(pl.multiple_of(p * block, block), block)
            d_keys_ref[dst, :] = key_sums[src, :].astype(d_keys_ref.dtype)
            return carry

        lax.fori_loop(0, blocks, restore, 0)


def attention(
    places, query_nope, query_rope, keys, key_rope, key_up, value_up, saved, upstream, logsum, group
):
    tokens = query_nope.shape[0]
    heads = query_nope.shape[1] // NOPE_DIM
    block = tokens // 2
    length = keys.shape[0]
    blocks = length // block
    rows = group * block
    totals = logsum.reshape(2, block, heads).transpose(0, 2, 1).reshape(2, 1, heads * block)
    whole = lambda i, places: (0, 0)
    part = lambda i, places: (0, i)
    pairs = length * heads * tokens // 2
    return pl.pallas_call(
        functools.partial(attention_kernel, group, block, blocks),
        grid_spec=pltpu.PrefetchScalarGridSpec(
            num_scalar_prefetch=1,
            grid=(heads // group,),
            in_specs=[
                pl.BlockSpec((tokens, group * NOPE_DIM), part),
                pl.BlockSpec((tokens, group * ROPE_DIM), part),
                pl.BlockSpec((length, LATENT), whole),
                pl.BlockSpec((length, ROPE_DIM), whole),
                pl.BlockSpec((LATENT, group * NOPE_DIM), part),
                pl.BlockSpec((LATENT, group * VALUE_DIM), part),
                pl.BlockSpec((tokens, group * LATENT), part),
                pl.BlockSpec((tokens, group * VALUE_DIM), part),
                pl.BlockSpec((2, 1, rows), lambda i, places: (0, 0, i)),
            ],
            out_specs=[
                pl.BlockSpec((tokens, group * NOPE_DIM), part),
                pl.BlockSpec((tokens, group * ROPE_DIM), part),
                pl.BlockSpec((length, WIDE), whole),
                pl.BlockSpec((LATENT, group * NOPE_DIM), part),
            ],
            scratch_shapes=[
                pltpu.VMEM((length, WIDE), jnp.bfloat16),
                pltpu.VMEM((length, WIDE), jnp.float32),
                pltpu.VMEM((2, rows, WIDE), jnp.bfloat16),
                pltpu.VMEM((2, rows, LATENT), jnp.bfloat16),
                pltpu.VMEM((2, 1, rows), jnp.float32),
                pltpu.VMEM((2, rows, WIDE), jnp.float32),
            ],
        ),
        out_shape=[
            jax.ShapeDtypeStruct(query_nope.shape, jnp.bfloat16),
            jax.ShapeDtypeStruct(query_rope.shape, jnp.bfloat16),
            jax.ShapeDtypeStruct((length, WIDE), jnp.bfloat16),
            jax.ShapeDtypeStruct((LATENT, heads * NOPE_DIM), jnp.bfloat16),
        ],
        compiler_params=pltpu.CompilerParams(vmem_limit_bytes=VMEM),
        cost_estimate=pl.CostEstimate(
            flops=pairs * 2 * 2752, bytes_accessed=20 * 1024 * 1024, transcendentals=pairs
        ),
        name="attention",
    )(places, query_nope, query_rope, keys, key_rope, key_up, value_up, saved, upstream, totals)


def local(
    query_nope,
    query_rope,
    latent,
    key_rope,
    key_up,
    value_up,
    latent_out,
    out_grad,
    logsum,
    block_order,
):
    axes = ("inner", "outer")
    heads = query_nope.shape[1] // NOPE_DIM
    blocks = block_order.shape[0]
    group = min(8, heads)
    all_keys = lax.all_gather(latent, axes, axis=0, tiled=True)
    all_rope = lax.all_gather(key_rope, axes, axis=0, tiled=True)
    index = lax.iota(jnp.int32, blocks)
    held = (block_order[:, None] == index[None, :]).astype(jnp.int32)
    stored = jnp.sum(held * index[:, None], axis=0)
    first = 2 * lax.axis_index(axes)
    own = lax.dynamic_slice_in_dim(block_order, first, 2, 0)
    places = jnp.concatenate([own, stored])
    value_weight = value_weights(latent_out, out_grad, group)
    d_value_up = lax.psum_scatter(value_weight, axes, scatter_dimension=0, tiled=True)
    d_nope, d_rope, d_keys, key_weight = attention(
        places,
        query_nope,
        query_rope,
        all_keys,
        all_rope,
        key_up,
        value_up,
        latent_out,
        out_grad,
        logsum,
        group,
    )
    own_keys = lax.psum_scatter(d_keys, axes, scatter_dimension=0, tiled=True)
    own_keys = lax.psum(own_keys, "head")
    d_key_up = lax.psum_scatter(key_weight, axes, scatter_dimension=0, tiled=True)
    return (
        d_nope,
        d_rope,
        own_keys[:, :LATENT],
        own_keys[:, LATENT : LATENT + ROPE_DIM],
        d_key_up.astype(jnp.float32),
        d_value_up.astype(jnp.float32),
    )


def solution(mesh):
    placed = (
        P(("inner", "outer"), "head"),
        P(("inner", "outer"), "head"),
        P(("inner", "outer"), None),
        P(("inner", "outer"), None),
        P(None, "head"),
        P(None, "head"),
        P(("inner", "outer"), "head"),
        P(("inner", "outer"), "head"),
        P(("inner", "outer"), "head"),
        P(),
    )
    return jax.shard_map(
        local,
        mesh=mesh,
        in_specs=placed,
        out_specs=(
            P(("inner", "outer"), "head"),
            P(("inner", "outer"), "head"),
            P(("inner", "outer"), None),
            P(("inner", "outer"), None),
            P(("inner", "outer"), "head"),
            P(("inner", "outer"), "head"),
        ),
        check_vma=False,
    )
```

time: 1160 us -> 364 us (0.31); the launches traced: 1140 us -> 364 us
  matrix products: 333 us -> 0 us
  starting transfers between devices: 243 us -> 0.2 us
  local copies, waits for them, and re-layouts: 197 us -> 6.08 us
  loops' own time: 98.5 us -> 0 us
  Pallas kernels: 0 us -> 68.2 us
  waiting for transfers between devices: 175 us -> 242 us
  other arithmetic: 69.9 us -> 4.88 us
  blocking collectives: 12.6 us -> 28.2 us
    dot_general x173 -> x0, matrix products: 333 us -> none  [the longest x42 150 us: contract_first(): lax.dot_general(first_op, second_op, (((0,), (0,)), ((), ())), preferred_...]
    ppermute x64 -> x0, starting transfers between devices: 243 us -> none  [shifted(): return lax.ppermute(block, axis, route)]
    reduce_scatter x2 -> x3, waiting for transfers between devices: 77.5 us -> 205 us  [the longest x1 74.8 us: local(): lax.psum_scatter(value_weight, axes, scatter_dimension=0, tiled=True)]
    another operation x33 -> x0, loops' own time: 98.5 us -> none  [the longest x1 97.2 us: local(): lax.fori_loop(0, context_size // 2, step_pair, ((latent, key_rope), start...]
    ppermute x64 -> x0, waiting for transfers between devices: 97 us -> none  [shifted(): return lax.ppermute(block, axis, route)]
    pallas_call x0 -> x2, Pallas kernels: none -> 68.2 us  [the longest x1 62.4 us: attention(): pl.pallas_call(functools.partial(attention_kernel, group, block, blocks),...]
    add x49 -> x0, other arithmetic: 51 us -> none  [the longest x32 45.5 us: step_pair(): key_sums = (key_sums[0] + contribution[0], key_sums[1] + contribution[1])]
    slice x42 -> x2, local copies, waits for them, and re-layouts: 43.4 us -> 2.33 us  [the longest x1 1.57 us: local(): own_keys[:, :LATENT]]
  transfers between devices with their start and end apart: 66 -> 5, of which waited for: 17 -> 5; matrix products, arithmetic and copies ran while one was open for 49% -> 3% of each run, Pallas kernels for 0% -> 2%
where the time goes in v1:
time: 364 us
  waiting for transfers between devices  242 us (66%)
  Pallas kernels  68.2 us (19%)
  blocking collectives  28.2 us (8%)
  between operations  13.8 us (4%)
  local copies, waits for them, and re-layouts  6.08 us (2%)
  other arithmetic  4.88 us (1%)
    reduce_scatter x1, waiting for transfers between devices, local(): lax.psum_scatter(value_weight, axes, scatter_dimension=0, tiled=True)  74.8 us
    reduce_scatter x1, waiting for transfers between devices, local(): lax.psum_scatter(key_weight, axes, scatter_dimension=0, tiled=True)  73.6 us
    pallas_call x1, Pallas kernels, attention(): pl.pallas_call(functools.partial(attention_kernel, group, block, blocks),...  62.4 us
    reduce_scatter x1, waiting for transfers between devices, local(): own_keys = lax.psum_scatter(d_keys, axes, scatter_dimension=0, tiled=True)  56.9 us
    all_gather x1, blocking collectives, local(): all_rope = lax.all_gather(key_rope, axes, axis=0, tiled=True)  28.2 us
    psum x1, waiting for transfers between devices, local(): own_keys = lax.psum(own_keys, 'head')  21.4 us
    all_gather x1, waiting for transfers between devices, local(): all_keys = lax.all_gather(latent, axes, axis=0, tiled=True)  14.3 us
  transfers between devices with their start and end apart: 5, of which 5 were waited for; matrix products, arithmetic and copies ran while one was open for 3% of the time, Pallas kernels for 2%

profile of v1, /device:TPU:0, one launch (start us, length us, event | category | flops | bytes accessed | tf_op | source)
XLA Modules:
  0.0 363.5 jit_solution(146733022881011247)
XLA Ops:
  7.2 0.0 all-gather.2.cloned.1.call-start
  7.2 0.7 all-gather.2.cloned.1.call-update
  7.9 0.0 reduce-scatter.4.cloned.1.call-start
  8.0 0.8 copy.19
  8.8 0.8 reshape.19
  9.6 0.7 reshape.20.logsum_ref
  10.3 0.7 dynamic_slice.3
  11.0 0.7 select_reduce_fusion
  11.8 0.6 pad_add_fusion.places_ref
  12.4 28.2 %all_gather.7.key_rope_ref = bf16[2048,64]{1,0:T(8,128)(2,1)} all-gather(bf16[128,64]{1,0:T(8,128)(2,1)S(1)} %copy.19), channel_id=1, replica_groups=mesh['head'=2,'inner'=2,'outer'=8] {'inner','outer'}, dimensions={0}, use_global_device_ids=true | all-gather | bytes 278528 | tf_op jit(solution)/shard_map/all_gather | solution.py:265
  40.6 14.3 %all-gather.2.cloned.1.call-done.lat_ref = bf16[2048,512]{1,0:T(8,128)(2,1)} async-done(((bf16[128,512]{1,0:T(8,128)(2,1)}), bf16[2048,512]{1,0:T(8,128)(2,1)}) %all-gather.2.cloned.1.call-update) | async-done | bytes 2097168 | tf_op jit(solution)/shard_map/all_gather | solution.py:264
  54.9 62.4 %attention.1 = (bf16[128,4096]{1,0:T(8,128)(2,1)}, bf16[128,2048]{1,0:T(8,128)(2,1)}, bf16[2048,640]{1,0:T(8,128)(2,1)}, bf16[512,4096]{1,0:T(8,128)(2,1)}) custom-call(s32[34]{0:T(128)} %pad_add_fusion.places_ref, bf16[128,4096]{1,0:T(8,128)(2,1)} %nope_ref.1, bf16[128,2048]{1,0:T(8,128)(2,1)} %rope_ref.1, ...), custom_call_target="tpu_custom_call" | custom-call | flops 23085449216 | bytes 20971520 | tf_op jit(solution)/shard_map/attention/pallas_call | solution.py:203
  117.3 0.0 reduce-scatter.4.cloned.1.call-update
  117.3 0.0 reduce-scatter.8.cloned.1.call-start
  117.4 5.8 %value_weights.1 = bf16[512,4096]{1,0:T(8,128)(2,1)} custom-call(bf16[128,16384]{1,0:T(8,128)(2,1)} %saved_ref.3, bf16[128,4096]{1,0:T(8,128)(2,1)} %upstream_ref.3), custom_call_target="tpu_custom_call" | custom-call | tf_op jit(solution)/shard_map/value_weights/pallas_call | solution.py:44
  123.2 0.0 reduce-scatter.8.cloned.1.call-update
  123.2 0.0 all-reduce.2.cloned.1.call-start
  123.3 56.9 %reduce-scatter.4.cloned.1.call-done = bf16[128,640]{1,0:T(8,128)(2,1)} async-done(((bf16[2048,640]{1,0:T(8,128)(2,1)}), bf16[128,640]{1,0:T(8,128)(2,1)}) %reduce-scatter.4.cloned.1.call-update) | async-done | bytes 163856 | tf_op jit(solution)/shard_map/reduce_scatter | solution.py:287
  180.1 0.0 all-reduce.2.cloned.1.call-update
  180.1 0.0 reduce-scatter.6.cloned.1.call-start
  180.2 0.5 reduce-scatter.6.cloned.1.call-update
  180.7 74.8 %reduce-scatter.8.cloned.1.call-done = bf16[32,4096]{1,0:T(8,128)(2,1)} async-done(((bf16[512,4096]{1,0:T(8,128)(2,1)}), bf16[32,4096]{1,0:T(8,128)(2,1)}) %reduce-scatter.8.cloned.1.call-update) | async-done | bytes 262160 | tf_op jit(solution)/shard_map/reduce_scatter | solution.py:273
  255.5 1.8 convert_element_type.8
  257.3 21.4 %all-reduce.2.cloned.1.call-done = bf16[128,640]{1,0:T(8,128)(2,1)} async-done(((bf16[128,640]{1,0:T(8,128)(2,1)}), bf16[128,640]{1,0:T(8,128)(2,1)}) %all-reduce.2.cloned.1.call-update) | async-done | bytes 163856 | tf_op jit(solution)/shard_map/psum | solution.py:288
  278.6 0.8 slice.9
  279.4 0.7 copy.21
  280.1 1.6 slice.8
  281.7 73.6 %reduce-scatter.6.cloned.1.call-done = bf16[32,4096]{1,0:T(8,128)(2,1)} async-done(((bf16[512,4096]{1,0:T(8,128)(2,1)}), bf16[32,4096]{1,0:T(8,128)(2,1)}) %reduce-scatter.6.cloned.1.call-update) | async-done | bytes 262160 | tf_op jit(solution)/shard_map/reduce_scatter | solution.py:289
  355.2 1.8 convert_element_type.7
  (1 shorter events, 0.0 us)
Async XLA Ops:
  7.2 47.7 %all-gather.2.cloned.1.call-start = ((), (), s32[]{:S(2)}) async-start(), calls=%async_computation.3 | async-start | bytes 2228224 | tf_op jit(solution)/shard_map/all_gather | solution.py:264
  7.9 172.2 %reduce-scatter.4.cloned.1.call-start = ((), (), s32[]{:S(2)}) async-start(), calls=%async_computation.4 | async-start | bytes 2785280 | tf_op jit(solution)/shard_map/reduce_scatter | solution.py:287
  117.3 138.2 %reduce-scatter.8.cloned.1.call-start = ((), (), s32[]{:S(2)}) async-start(), calls=%async_computation.7 | async-start | bytes 4456448 | tf_op jit(solution)/shard_map/reduce_scatter | solution.py:273
  123.2 155.4 %all-reduce.2.cloned.1.call-start = ((), (), s32[]{:S(2)}) async-start(), calls=%async_computation.5 | async-start | bytes 327680 | tf_op jit(solution)/shard_map/psum | solution.py:288
  180.1 175.1 %reduce-scatter.6.cloned.1.call-start = ((), (), s32[]{:S(2)}) async-start(), calls=%async_computation.6 | async-start | bytes 4456448 | tf_op jit(solution)/shard_map/reduce_scatter | solution.py:289
Sparse Core Ops, SparseCore 0:
  10.2 44.6 all-gather.1
  117.5 62.6 reduce-scatter.3
  184.0 71.4 reduce-scatter.7
  257.7 20.8 all-reduce.1
  282.8 72.3 reduce-scatter.5

commit v2 on v1

--- a/solution.py
+++ b/solution.py
@@ -63,7 +63,6 @@
     nope_ref,
     rope_ref,
     lat_ref,
-    key_rope_ref,
     key_up_ref,
     value_up_ref,
     saved_ref,
@@ -89,9 +88,7 @@
         def sort(p, carry):
             src = pl.ds(pl.multiple_of(places_ref[2 + p] * block, block), block)
             dst = pl.ds(pl.multiple_of(p * block, block), block)
-            keys[dst, :LATENT] = lat_ref[src, :]
-            part = key_rope_ref[src, :]
-            keys[dst, LATENT:] = jnp.concatenate([part, jnp.zeros_like(part)], axis=1)
+            keys[dst, :] = lat_ref[src, :]
             return carry
 
         lax.fori_loop(0, blocks, sort, 0)
@@ -188,7 +185,7 @@
 
 
 def attention(
-    places, query_nope, query_rope, keys, key_rope, key_up, value_up, saved, upstream, logsum, group
+    places, query_nope, query_rope, keys, key_up, value_up, saved, upstream, logsum, group
 ):
     tokens = query_nope.shape[0]
     heads = query_nope.shape[1] // NOPE_DIM
@@ -208,8 +205,7 @@
             in_specs=[
                 pl.BlockSpec((tokens, group * NOPE_DIM), part),
                 pl.BlockSpec((tokens, group * ROPE_DIM), part),
-                pl.BlockSpec((length, LATENT), whole),
-                pl.BlockSpec((length, ROPE_DIM), whole),
+                pl.BlockSpec((length, WIDE), whole),
                 pl.BlockSpec((LATENT, group * NOPE_DIM), part),
                 pl.BlockSpec((LATENT, group * VALUE_DIM), part),
                 pl.BlockSpec((tokens, group * LATENT), part),
@@ -242,7 +238,382 @@
             flops=pairs * 2 * 2752, bytes_accessed=20 * 1024 * 1024, transcendentals=pairs
         ),
         name="attention",
-    )(places, query_nope, query_rope, keys, key_rope, key_up, value_up, saved, upstream, totals)
+    )(places, query_nope, query_rope, keys, key_up, value_up, saved, upstream, totals)
+
+
+MESH = pl.DeviceIdType.MESH
+
+
+def device_at(place, axis, value):
+    head, inner, outer = place
+    if axis == "head":
+        return (value, inner, outer)
+    if axis == "inner":
+        return (head, value, outer)
+    if axis == "depth":
+        return (head, inner, value * 2 + lax.rem(outer, 2))
+    return (head, inner, outer - lax.rem(outer, 2) + value)
+
+
+def where_am_i():
+    head, inner, outer = (lax.axis_index(a) for a in ("head", "inner", "outer"))
+    spot = {"head": head, "inner": inner, "depth": outer // 2, "core": lax.rem(outer, 2)}
+    return (head, inner, outer), spot
+
+
+def greet(place, spot, sizes, axes):
+    barrier = pltpu.get_barrier_semaphore()
+    count = 0
+    for axis in axes:
+        for k in range(1, sizes[axis]):
+            target = lax.rem(spot[axis] + k, sizes[axis])
+            pl.semaphore_signal(
+                barrier, inc=1, device_id=device_at(place, axis, target), device_id_type=MESH
+            )
+            count += 1
+    pl.semaphore_wait(barrier, count)
+
+
+def gather_kernel(sizes, own_ref, out_ref, *sems):
+    deep_send, deep_recv, side_send, side_recv, core_send, core_recv = sems
+    place, spot = where_am_i()
+    depth, sides = sizes["depth"], sizes["inner"]
+    greet(place, spot, sizes, ("core", "depth", "inner"))
+    inner, level, core = spot["inner"], spot["depth"], spot["core"]
+    out_ref[inner, level, core] = own_ref[...]
+    started = []
+
+    def send(slot, axis, target, send_sem, recv_sem):
+        copy = pltpu.make_async_remote_copy(
+            src_ref=out_ref.at[slot],
+            dst_ref=out_ref.at[slot],
+            send_sem=send_sem,
+            recv_sem=recv_sem,
+            device_id=device_at(place, axis, target),
+            device_id_type=MESH,
+        )
+        copy.start()
+        started.append(copy)
+        return copy
+
+    def to_core(k, j):
+        slot = (lax.rem(inner + sides - k, sides), lax.rem(level + depth - j, depth), core)
+        return send(slot, "core", 1 - core, core_send.at[k, j], core_recv.at[k, j])
+
+    def to_sides(j):
+        slot = (inner, lax.rem(level + depth - j, depth), core)
+        return [
+            send(
+                slot,
+                "inner",
+                lax.rem(inner + k, sides),
+                side_send.at[k - 1, j],
+                side_recv.at[k - 1, j],
+            )
+            for k in range(1, sides)
+        ]
+
+    deep = [
+        send(
+            (inner, level, core),
+            "depth",
+            lax.rem(level + k, depth),
+            deep_send.at[k - 1],
+            deep_recv.at[k - 1],
+        )
+        for k in range(1, depth)
+    ]
+    side = [to_sides(0)]
+    last = [to_core(0, 0)]
+    for j in range(1, depth):
+        deep[j - 1].wait_recv()
+        side.append(to_sides(j))
+        last.append(to_core(0, j))
+    for j in range(depth):
+        for k in range(1, sides):
+            side[j][k - 1].wait_recv()
+            last.append(to_core(k, j))
+    for copy in last:
+        copy.wait_recv()
+    for copy in started:
+        copy.wait_send()
+
+
+def gather_rows(own, sizes):
+    depth, sides = sizes["depth"], sizes["inner"]
+    dma = pltpu.SemaphoreType.DMA
+    return pl.pallas_call(
+        functools.partial(gather_kernel, sizes),
+        in_specs=[pl.BlockSpec(memory_space=pltpu.VMEM)],
+        out_specs=pl.BlockSpec(memory_space=pltpu.VMEM),
+        out_shape=jax.ShapeDtypeStruct((sides, depth, 2) + own.shape, own.dtype),
+        scratch_shapes=[
+            dma((depth - 1,)),
+            dma((depth - 1,)),
+            dma((sides - 1, depth)),
+            dma((sides - 1, depth)),
+            dma((sides, depth)),
+            dma((sides, depth)),
+        ],
+        compiler_params=pltpu.CompilerParams(
+            collective_id=0, has_side_effects=True, vmem_limit_bytes=VMEM
+        ),
+        name="gather_keys",
+    )(own)
+
+
+def wide(x):
+    return x.astype(jnp.float32)
+
+
+def reduce_kernel(
+    sizes,
+    pieces,
+    weight_ref,
+    keys_ref,
+    out_weight_ref,
+    out_keys_ref,
+    w_recv1,
+    w_sum1,
+    w_recv2,
+    w_sum2,
+    w_recv3,
+    k_recv1,
+    k_sum1,
+    k_recv2,
+    k_sum2,
+    k_recv3,
+    k_sum3,
+    k_recv4,
+    w1_send,
+    w1_recv,
+    w2_send,
+    w2_recv,
+    w3_send,
+    w3_recv,
+    k1_send,
+    k1_recv,
+    k2_send,
+    k2_recv,
+    k3_send,
+    k3_recv,
+    k4_send,
+    k4_recv,
+    k5_send,
+    k5_recv,
+):
+    place, spot = where_am_i()
+    depth, sides, heads = sizes["depth"], sizes["inner"], sizes["head"]
+    greet(place, spot, sizes, ("core", "depth", "inner", "head"))
+    inner, level, core, head = (spot[a] for a in ("inner", "depth", "core", "head"))
+    width = weight_ref.shape[-1] // pieces
+    share = keys_ref.shape[-2] // heads
+    started = []
+
+    def send(src, dst, axis, target, send_sem, recv_sem):
+        copy = pltpu.make_async_remote_copy(
+            src_ref=src,
+            dst_ref=dst,
+            send_sem=send_sem,
+            recv_sem=recv_sem,
+            device_id=device_at(place, axis, target),
+            device_id_type=MESH,
+        )
+        copy.start()
+        started.append(copy)
+        return copy
+
+    def scatter(axis, source, target_buffer, sends, recvs):
+        out = []
+        for k in range(1, sizes[axis]):
+            target = lax.rem(spot[axis] + k, sizes[axis])
+            out.append(
+                send(
+                    source(target), target_buffer(k - 1), axis, target, sends(k - 1), recvs(k - 1)
+                )
+            )
+        return out
+
+    def arrive(copies):
+        for copy in copies:
+            copy.wait_recv()
+
+    keys_copy = send(keys_ref.at[:, :, 1 - core], k_recv1, "core", 1 - core, k1_send, k1_recv)
+    cols = [slice(c * width, (c + 1) * width) for c in range(pieces)]
+    first = [
+        send(
+            weight_ref.at[:, :, 1 - core, :, cols[c]],
+            w_recv1.at[c],
+            "core",
+            1 - core,
+            w1_send.at[c],
+            w1_recv.at[c],
+        )
+        for c in range(pieces)
+    ]
+    keys_copy.wait_recv()
+    for i in range(sides):
+        for j in range(depth):
+            k_sum1[i, j] = (wide(keys_ref[i, j, core]) + wide(k_recv1[i, j])).astype(k_sum1.dtype)
+
+    def rows_of(target):
+        return pl.ds(pl.multiple_of(target * share, share), share)
+
+    k_heads = scatter(
+        "head",
+        lambda p: k_sum1.at[:, :, rows_of(p), :],
+        lambda k: k_recv2.at[k],
+        lambda k: k2_send.at[k],
+        lambda k: k2_recv.at[k],
+    )
+    second = []
+    for c in range(pieces):
+        first[c].wait_recv()
+        for i in range(sides):
+            for j in range(depth):
+                w_sum1[c, i, j] = (
+                    wide(weight_ref[i, j, core, :, cols[c]]) + wide(w_recv1[c, i, j])
+                ).astype(w_sum1.dtype)
+        second.append(
+            scatter(
+                "inner",
+                lambda p: w_sum1.at[c, p],
+                lambda k: w_recv2.at[c, k],
+                lambda k: w2_send.at[c, k],
+                lambda k: w2_recv.at[c, k],
+            )
+        )
+    arrive(k_heads)
+    for i in range(sides):
+        for j in range(depth):
+            total = wide(k_sum1[i, j, rows_of(head), :])
+            for k in range(heads - 1):
+                total = total + wide(k_recv2[k, i, j])
+            k_sum2[i, j] = total.astype(k_sum2.dtype)
+    k_sides = scatter(
+        "inner",
+        lambda p: k_sum2.at[p],
+        lambda k: k_recv3.at[k],
+        lambda k: k3_send.at[k],
+        lambda k: k3_recv.at[k],
+    )
+    third = []
+
+    def middle(c):
+        arrive(second[c])
+        for j in range(depth):
+            total = wide(w_sum1[c, inner, j])
+            for k in range(sides - 1):
+                total = total + wide(w_recv2[c, k, j])
+            w_sum2[c, j] = total.astype(w_sum2.dtype)
+        third.append(
+            scatter(
+                "depth",
+                lambda p: w_sum2.at[c, p],
+                lambda k: w_recv3.at[c, k],
+                lambda k: w3_send.at[c, k],
+                lambda k: w3_recv.at[c, k],
+            )
+        )
+
+    for c in range(pieces - 1):
+        middle(c)
+    arrive(k_sides)
+    for j in range(depth):
+        total = wide(k_sum2[inner, j])
+        for k in range(sides - 1):
+            total = total + wide(k_recv3[k, j])
+        k_sum3[j] = total.astype(k_sum3.dtype)
+    k_depth = scatter(
+        "depth",
+        lambda p: k_sum3.at[p],
+        lambda k: k_recv4.at[k],
+        lambda k: k4_send.at[k],
+        lambda k: k4_recv.at[k],
+    )
+    middle(pieces - 1)
+    arrive(k_depth)
+    total = wide(k_sum3[level])
+    for k in range(depth - 1):
+        total = total + wide(k_recv4[k])
+    out_keys_ref[rows_of(head), :] = total.astype(out_keys_ref.dtype)
+    k_last = [
+        send(
+            out_keys_ref.at[rows_of(head), :],
+            out_keys_ref.at[rows_of(head), :],
+            "head",
+            lax.rem(head + k, heads),
+            k5_send.at[k - 1],
+            k5_recv.at[k - 1],
+        )
+        for k in range(1, heads)
+    ]
+    for c in range(pieces):
+        arrive(third[c])
+        total = wide(w_sum2[c, level])
+        for k in range(depth - 1):
+            total = total + wide(w_recv3[c, k])
+        out_weight_ref[:, cols[c]] = total
+    arrive(k_last)
+    for copy in started:
+        copy.wait_send()
+
+
+def reduce_rows(weight, keys, sizes, pieces):
+    depth, sides, heads = sizes["depth"], sizes["inner"], sizes["head"]
+    owners = sides * depth * 2
+    rows, width = weight.shape[0] // owners, weight.shape[1]
+    tokens = keys.shape[0] // owners
+    weight = weight.reshape(sides, depth, 2, rows, width)
+    keys = keys.reshape(sides, depth, 2, tokens, keys.shape[1])
+    piece = (rows, width // pieces)
+    whole = (tokens, WIDE)
+    part = (tokens // heads, WIDE)
+    vmem = lambda *shape: pltpu.VMEM(shape, jnp.bfloat16)
+    dma = pltpu.SemaphoreType.DMA
+    return pl.pallas_call(
+        functools.partial(reduce_kernel, sizes, pieces),
+        in_specs=[pl.BlockSpec(memory_space=pltpu.VMEM)] * 2,
+        out_specs=[pl.BlockSpec(memory_space=pltpu.VMEM)] * 2,
+        out_shape=[
+            jax.ShapeDtypeStruct((rows, width), jnp.float32),
+            jax.ShapeDtypeStruct(whole, jnp.bfloat16),
+        ],
+        scratch_shapes=[
+            vmem(pieces, sides, depth, *piece),
+            vmem(pieces, sides, depth, *piece),
+            vmem(pieces, sides - 1, depth, *piece),
+            vmem(pieces, depth, *piece),
+            vmem(pieces, depth - 1, *piece),
+            vmem(sides, depth, *whole),
+            vmem(sides, depth, *whole),
+            vmem(heads - 1, sides, depth, *part),
+            vmem(sides, depth, *part),
+            vmem(sides - 1, depth, *part),
+            vmem(depth, *part),
+            vmem(depth - 1, *part),
+            dma((pieces,)),
+            dma((pieces,)),
+            dma((pieces, sides - 1)),
+            dma((pieces, sides - 1)),
+            dma((pieces, depth - 1)),
+            dma((pieces, depth - 1)),
+            dma(()),
+            dma(()),
+            dma((heads - 1,)),
+            dma((heads - 1,)),
+            dma((sides - 1,)),
+            dma((sides - 1,)),
+            dma((depth - 1,)),
+            dma((depth - 1,)),
+            dma((heads - 1,)),
+            dma((heads - 1,)),
+        ],
+        compiler_params=pltpu.CompilerParams(
+            collective_id=1, has_side_effects=True, vmem_limit_bytes=VMEM
+        ),
+        name="reduce_gradients",
+    )(weight, keys)
 
 
 def local(
@@ -261,22 +632,28 @@
     heads = query_nope.shape[1] // NOPE_DIM
     blocks = block_order.shape[0]
     group = min(8, heads)
-    all_keys = lax.all_gather(latent, axes, axis=0, tiled=True)
-    all_rope = lax.all_gather(key_rope, axes, axis=0, tiled=True)
+    sizes = {
+        "head": lax.axis_size("head"),
+        "inner": lax.axis_size("inner"),
+        "depth": lax.axis_size("outer") // 2,
+        "core": 2,
+    }
+    value_weight = value_weights(latent_out, out_grad, group)
+    d_value_up = lax.psum_scatter(value_weight, axes, scatter_dimension=0, tiled=True)
+    own_keys = jnp.concatenate([latent, key_rope, jnp.zeros_like(key_rope)], axis=1)
+    own_keys, value_weight = lax.optimization_barrier((own_keys, value_weight))
+    all_keys = gather_rows(own_keys, sizes).reshape(-1, WIDE)
     index = lax.iota(jnp.int32, blocks)
     held = (block_order[:, None] == index[None, :]).astype(jnp.int32)
     stored = jnp.sum(held * index[:, None], axis=0)
     first = 2 * lax.axis_index(axes)
     own = lax.dynamic_slice_in_dim(block_order, first, 2, 0)
     places = jnp.concatenate([own, stored])
-    value_weight = value_weights(latent_out, out_grad, group)
-    d_value_up = lax.psum_scatter(value_weight, axes, scatter_dimension=0, tiled=True)
     d_nope, d_rope, d_keys, key_weight = attention(
         places,
         query_nope,
         query_rope,
         all_keys,
-        all_rope,
         key_up,
         value_up,
         latent_out,
@@ -284,15 +661,13 @@
         logsum,
         group,
     )
-    own_keys = lax.psum_scatter(d_keys, axes, scatter_dimension=0, tiled=True)
-    own_keys = lax.psum(own_keys, "head")
-    d_key_up = lax.psum_scatter(key_weight, axes, scatter_dimension=0, tiled=True)
+    d_key_up, own_sums = reduce_rows(key_weight, d_keys, sizes, 4)
     return (
         d_nope,
         d_rope,
-        own_keys[:, :LATENT],
-        own_keys[:, LATENT : LATENT + ROPE_DIM],
-        d_key_up.astype(jnp.float32),
+        own_sums[:, :LATENT],
+        own_sums[:, LATENT : LATENT + ROPE_DIM],
+        d_key_up,
         d_value_up.astype(jnp.float32),
     )
 

time: 364 us -> 182 us (0.50)
  waiting for transfers between devices: 242 us -> 0.02 us
  Pallas kernels: 68.2 us -> 157 us
  blocking collectives: 28.2 us -> 0 us
    reduce_scatter x2 -> x0, waiting for transfers between devices: 130 us -> none  [the longest x1 73.6 us: local(): lax.psum_scatter(key_weight, axes, scatter_dimension=0, tiled=True)]
    pallas_call x0 -> x2, Pallas kernels: none -> 89 us  [the longest x1 59.6 us: reduce_rows(): pl.pallas_call(functools.partial(reduce_kernel, sizes, pieces), in_specs=...]
    reduce_scatter x1, waiting for transfers between devices: 74.8 us -> 0.01 us  [local(): lax.psum_scatter(value_weight, axes, scatter_dimension=0, tiled=True)]
    all_gather x1 -> x0, blocking collectives: 28.2 us -> none  [local(): all_rope = lax.all_gather(key_rope, axes, axis=0, tiled=True)]
    psum x1 -> x0, waiting for transfers between devices: 21.4 us -> none  [local(): own_keys = lax.psum(own_keys, 'head')]
    all_gather x1 -> x0, waiting for transfers between devices: 14.3 us -> none  [local(): all_keys = lax.all_gather(latent, axes, axis=0, tiled=True)]
  transfers between devices with their start and end apart: 5 -> 1, of which waited for: 5 -> 0; matrix products, arithmetic and copies ran while one was open for 3% -> 3% of each run, Pallas kernels for 2% -> 84%
where the time goes in v2:
time: 182 us; the launch traced here: 181 us
  Pallas kernels  157 us (86%)
  between operations  14.1 us (8%)
  local copies, waits for them, and re-layouts  6.62 us (4%)
  other arithmetic  3.15 us (2%)
    pallas_call x1, Pallas kernels, attention(): pl.pallas_call(functools.partial(attention_kernel, group, block, blocks),...  62.6 us
    pallas_call x1, Pallas kernels, reduce_rows(): pl.pallas_call(functools.partial(reduce_kernel, sizes, pieces), in_specs=...  59.6 us
    pallas_call x1, Pallas kernels, gather_rows(): pl.pallas_call(functools.partial(gather_kernel, sizes), in_specs=[pl.Bloc...  29.4 us
    pallas_call x1, Pallas kernels, value_weights(): pl.pallas_call(functools.partial(value_kernel, group), grid=(heads // gro...  5.75 us
  transfers between devices with their start and end apart: 1, of which 0 were waited for; matrix products, arithmetic and copies ran while one was open for 3% of the time, Pallas kernels for 84%

profile of v2, /device:TPU:0, one launch (start us, length us, event | category | flops | bytes accessed | tf_op | source)
XLA Modules:
  0.0 181.2 jit_solution(11039981140216898965)
XLA Ops:
  7.2 0.0 reduce-scatter.2.cloned.1.call-start
  7.2 5.7 %value_weights.1 = bf16[512,4096]{1,0:T(8,128)(2,1)} custom-call(bf16[128,16384]{1,0:T(8,128)(2,1)} %saved_ref.3, bf16[128,4096]{1,0:T(8,128)(2,1)} %upstream_ref.3), custom_call_target="tpu_custom_call" | custom-call | tf_op jit(solution)/shard_map/value_weights/pallas_call | solution.py:44
  13.0 0.0 copy-start.1
  13.0 0.0 copy-start.2
  13.0 0.0 copy-start
  13.0 0.0 copy-start.3
  13.0 0.0 reduce-scatter.2.cloned.1.call-update
  13.0 0.7 copy-done.1
  13.7 0.1 copy.19
  13.8 0.0 copy-done.2
  13.8 0.1 reshape.29
  13.9 0.7 reshape.30.logsum_ref
  14.6 0.1 pad.2.clone
  14.7 0.0 copy-done
  14.7 0.7 maximum_maximum_fusion.own_ref
  15.4 29.4 %gather_keys.1 = bf16[2,4,2,128,640]{4,3,2,1,0:T(8,128)(2,1)} custom-call(bf16[128,640]{1,0:T(8,128)(2,1)} %maximum_maximum_fusion.own_ref), custom_call_target="tpu_custom_call" | custom-call | tf_op jit(solution)/shard_map/gather_keys/pallas_call | solution.py:345
  44.8 0.0 copy-done.3
  44.8 0.1 dynamic_slice.3
  44.9 0.1 select_reduce_fusion
  45.0 0.6 pad_add_fusion.places_ref
  45.6 62.6 %attention.1 = (bf16[128,4096]{1,0:T(8,128)(2,1)}, bf16[128,2048]{1,0:T(8,128)(2,1)}, bf16[2048,640]{1,0:T(8,128)(2,1)}, bf16[512,4096]{1,0:T(8,128)(2,1)}) custom-call(s32[34]{0:T(128)} %pad_add_fusion.places_ref, bf16[128,4096]{1,0:T(8,128)(2,1)} %nope_ref.1, bf16[128,2048]{1,0:T(8,128)(2,1)} %rope_ref.1, bf16[2048,640]{1,0:T(8,128)(2,1)} %bitcast.9, ...), custom_call_target="tpu_custom_call" | custom-call | flops 23085449216 | bytes 20971520 | tf_op jit(solution)/shard_map/attention/pallas_call | solution.py:200
  108.1 59.6 %reduce_gradients.1 = (f32[32,4096]{1,0:T(8,128)}, bf16[128,640]{1,0:T(8,128)(2,1)}) custom-call(bf16[2,4,2,32,4096]{4,3,2,1,0:T(8,128)(2,1)} %bitcast.8, bf16[2,4,2,128,640]{4,3,2,1,0:T(8,128)(2,1)} %bitcast.10), custom_call_target="tpu_custom_call" | custom-call | tf_op jit(solution)/shard_map/reduce_gradients/pallas_call | solution.py:574
  167.7 0.8 slice.7
  168.5 1.6 slice.6
  170.0 0.7 copy.21
  170.7 0.0 reduce-scatter.2.cloned.1.call-done
  170.7 1.8 convert_element_type.4
  172.5 1.9 %copy.25 = f32[32,4096]{1,0:T(8,128)} copy(f32[32,4096]{1,0:T(8,128)} %get-tuple-element.42) | data formatting | bytes 1048576
  (2 shorter events, 0.0 us)
Async XLA Ops:
  7.2 163.6 %reduce-scatter.2.cloned.1.call-start = ((), (), s32[]{:S(2)}) async-start(), calls=%async_computation.1 | async-start | bytes 4456448 | tf_op jit(solution)/shard_map/reduce_scatter | solution.py:642
  13.0 0.7 copy-start.1
  13.0 0.8 copy-start.2
  13.0 1.7 copy-start
  13.0 31.8 %copy-start.3 = (s32[32]{0:T(128)S(1)}, s32[32]{0:T(128)}, u32[]{:S(2)}) copy-start(s32[32]{0:T(128)} %param.19) | copy-start | bytes 388
Sparse Core Ops, SparseCore 0:
  13.1 75.4 reduce-scatter.1

commit v3 on v1

v3 whole, which is shorter than its diff:
```python
import functools

import jax
import jax.numpy as jnp
from jax import lax
from jax.experimental import pallas as pl
from jax.experimental.pallas import tpu as pltpu
from jax.sharding import PartitionSpec as P

LATENT = 512
ROPE_DIM = 64
NOPE_DIM = 128
VALUE_DIM = 128
WIDE = 640
SPAN = 4
STORED = 2
FACTOR = float(NOPE_DIM + ROPE_DIM) ** (-0.5)
VMEM = 60 * 1024 * 1024


def contract_last(first_op, second_op):
    return lax.dot_general(
        first_op, second_op, (((1,), (1,)), ((), ())), preferred_element_type=jnp.float32
    )


def contract_first(first_op, second_op):
    return lax.dot_general(
        first_op, second_op, (((0,), (0,)), ((), ())), preferred_element_type=jnp.float32
    )


MESH = pl.DeviceIdType.MESH


def device_at(place, axis, value):
    head, inner, outer = place
    if axis == "head":
        return (value, inner, outer)
    if axis == "inner":
        return (head, value, outer)
    if axis == "depth":
        return (head, inner, value * 2 + lax.rem(outer, 2))
    return (head, inner, outer - lax.rem(outer, 2) + value)


def where_am_i():
    head, inner, outer = (lax.axis_index(a) for a in ("head", "inner", "outer"))
    spot = {"head": head, "inner": inner, "depth": outer // 2, "core": lax.rem(outer, 2)}
    return (head, inner, outer), spot


def greet(place, spot, sizes, axes):
    barrier = pltpu.get_barrier_semaphore()
    count = 0
    for axis in axes:
        for k in range(1, sizes[axis]):
            target = lax.rem(spot[axis] + k, sizes[axis])
            pl.semaphore_signal(
                barrier, inc=1, device_id=device_at(place, axis, target), device_id_type=MESH
            )
            count += 1
    pl.semaphore_wait(barrier, count)


def wide(x):
    return x.astype(jnp.float32)


def fused_kernel(
    sizes,
    group,
    block,
    blocks,
    places_ref,
    own_ref,
    nope_ref,
    rope_ref,
    key_up_ref,
    value_up_ref,
    saved_ref,
    upstream_ref,
    logsum_ref,
    d_nope_ref,
    d_rope_ref,
    d_latent_ref,
    d_key_rope_ref,
    d_key_up_ref,
    d_value_up_ref,
    gathered,
    keys,
    slots,
    queries,
    grads,
    delta,
    query_sums,
    w_part,
    w_recv1,
    w_recv2,
    w_sum2,
    w_recv3,
    k_part,
    k_recv1,
    k_recv2,
    k_sum2,
    k_recv3,
    k_sum3,
    k_recv4,
    k_own,
    g_depth,
    g_side,
    g_core,
    w1,
    w2,
    w3,
    k1,
    k2,
    k3,
    k4,
    k5,
):
    place, spot = where_am_i()
    depth, sides, heads = sizes["depth"], sizes["inner"], sizes["head"]
    inner, level, core, head = (spot[a] for a in ("inner", "depth", "core", "head"))
    rows = group * block
    tile = SPAN * block
    tiles = blocks // SPAN
    width = group * NOPE_DIM
    share = 2 * block // heads
    step = pl.program_id(0)
    steps = pl.num_programs(0)

    def remote(src, dst, axis, target, sems):
        return pltpu.make_async_remote_copy(
            src_ref=src,
            dst_ref=dst,
            send_sem=sems[0],
            recv_sem=sems[1],
            device_id=device_at(place, axis, target),
            device_id_type=MESH,
        )

    def partner(axis, k):
        return lax.rem(spot[axis] + k, sizes[axis])

    def both(sems, *index):
        return sems.at[(0,) + index], sems.at[(1,) + index]

    def owned(i, j, c):
        return pl.ds(2 * ((i * depth + j) * 2 + c), 2)

    def slot_copy(slot, axis, target, sems):
        both_blocks = gathered.at[owned(*slot)]
        return remote(both_blocks, both_blocks, axis, target, sems)

    def depth_key(k):
        return slot_copy((inner, level, core), "depth", partner("depth", k), both(g_depth, k - 1))

    def side_key(k, j):
        slot = (inner, lax.rem(level + depth - j, depth), core)
        return slot_copy(slot, "inner", partner("inner", k), both(g_side, k - 1, j))

    def core_key(k, j):
        slot = (lax.rem(inner + sides - k, sides), lax.rem(level + depth - j, depth), core)
        return slot_copy(slot, "core", 1 - core, both(g_core, k, j))

    def weight_core(kind, g):
        return remote(
            w_part.at[kind, g, :, :, 1 - core],
            w_recv1.at[kind, g],
            "core",
            1 - core,
            both(w1, kind, g),
        )

    def weight_side(kind, g, k):
        p = partner("inner", k)
        return remote(
            w_recv1.at[kind, g, p],
            w_recv2.at[kind, g, k - 1],
            "inner",
            p,
            both(w2, kind, g, k - 1),
        )

    def weight_depth(kind, g, k):
        p = partner("depth", k)
        return remote(
            w_sum2.at[kind, g, p],
            w_recv3.at[kind, g, k - 1],
            "depth",
            p,
            both(w3, kind, g, k - 1),
        )

    def start_weight(kind, g):
        weight_core(kind, g).start()

    def to_side(kind, g):
        weight_core(kind, g).wait_recv()
        for i in range(sides):
            for j in range(depth):
                total = wide(w_part[kind, g, i, j, core]) + wide(w_recv1[kind, g, i, j])
                w_recv1[kind, g, i, j] = total.astype(w_recv1.dtype)
        for k in range(1, sides):
            weight_side(kind, g, k).start()

    def to_depth(kind, g):
        for k in range(1, sides):
            weight_side(kind, g, k).wait_recv()
        for j in range(depth):
            total = wide(w_recv1[kind, g, inner, j])
            for k in range(sides - 1):
                total = total + wide(w_recv2[kind, g, k, j])
            w_sum2[kind, g, j] = total.astype(w_sum2.dtype)
        for k in range(1, depth):
            weight_depth(kind, g, k).start()

    def finish_weight(kind, g, out_ref):
        for k in range(1, depth):
            weight_depth(kind, g, k).wait_recv()
        total = wide(w_sum2[kind, g, level])
        for k in range(depth - 1):
            total = total + wide(w_recv3[kind, g, k])
        out_ref[:, pl.ds(pl.multiple_of(g * width, width), width)] = total

    def finish_sends(kind, g):
        weight_core(kind, g).wait_send()
        for k in range(1, sides):
            weight_side(kind, g, k).wait_send()
        for k in range(1, depth):
            weight_depth(kind, g, k).wait_send()

    def put_weight(kind, h, value):
        shaped = value.astype(w_part.dtype).reshape(w_part.shape[2:6] + (NOPE_DIM,))
        w_part[kind, step, :, :, :, :, h * NOPE_DIM : (h + 1) * NOPE_DIM] = shaped

    @pl.when(step == 0)
    def _():
        greet(place, spot, sizes, ("core", "depth", "inner", "head"))
        gathered[owned(inner, level, core)] = own_ref[...].reshape(2, block, WIDE)
        for k in range(1, depth):
            depth_key(k).start()
        for k in range(1, sides):
            side_key(k, 0).start()
        core_key(0, 0).start()
        slots[...] = jnp.zeros_like(slots)

    for h in range(group):
        saved = saved_ref[:, h * LATENT : (h + 1) * LATENT]
        upstream = upstream_ref[:, h * VALUE_DIM : (h + 1) * VALUE_DIM]
        put_weight(0, h, contract_first(saved, upstream))
    start_weight(0, step)

    @pl.when(step == 0)
    def _():
        for j in range(1, depth):
            depth_key(j).wait_recv()
            for k in range(1, sides):
                side_key(k, j).start()
            core_key(0, j).start()

    @pl.when(step > 0)
    def _():
        to_side(1, step - 1)

    query_sums[...] = jnp.zeros_like(query_sums)
    for h in range(group):
        nope = nope_ref[:, h * NOPE_DIM : (h + 1) * NOPE_DIM]
        key_map = key_up_ref[:, h * NOPE_DIM : (h + 1) * NOPE_DIM]
        lat = contract_last(nope, key_map).astype(jnp.bfloat16)
        upstream = upstream_ref[:, h * VALUE_DIM : (h + 1) * VALUE_DIM]
        value_map = value_up_ref[:, h * VALUE_DIM : (h + 1) * VALUE_DIM]
        grad = contract_last(upstream, value_map).astype(jnp.bfloat16)
        for t in range(2):
            mine = slice(h * block, (h + 1) * block)
            held = slice(t * block, (t + 1) * block)
            queries[t, mine, :LATENT] = lat[held]
            part = rope_ref[held, h * ROPE_DIM : (h + 1) * ROPE_DIM]
            queries[t, mine, LATENT:] = jnp.concatenate([part, jnp.zeros_like(part)], axis=1)
            grads[t, mine, :] = grad[held]
    for t in range(2):
        held = slice(t * block, (t + 1) * block)
        for h in range(0, group, 2):
            saved = jnp.concatenate(
                [saved_ref[held, k * LATENT : (k + 1) * LATENT] for k in (h, h + 1)], axis=0
            )
            mine = slice(h * block, (h + 2) * block)
            product = wide(grads[t, mine, :]) * wide(saved)
            folded = product[:, :128]
            for k in range(128, LATENT, 128):
                folded = folded + product[:, k : k + 128]
            delta[t, :, mine] = jnp.sum(folded.T, axis=0, keepdims=True)

    @pl.when(step == 0)
    def _():
        for j in range(depth):
            for k in range(1, sides):
                side_key(k, j).wait_recv()
                core_key(k, j).start()
        for j in range(depth):
            for k in range(sides):
                core_key(k, j).wait_recv()

        def sort(p, carry):
            for k in range(SPAN):
                keys[p, k * block : (k + 1) * block, :] = gathered[
                    places_ref[STORED + p * SPAN + k]
                ]
            return carry

        lax.fori_loop(0, tiles, sort, 0)

    to_side(0, step)

    span = tiles + 1
    base = STORED + 2 * blocks
    late = places_ref[0]
    early = places_ref[1]
    key_index = lax.broadcasted_iota(jnp.int32, (tile, rows), 0)
    row_index = lax.rem(lax.broadcasted_iota(jnp.int32, (tile, rows), 1), block)
    apart = key_index - row_index

    def visit(i, carry):
        target = places_ref[base + i]
        upper = jnp.broadcast_to(places_ref[base + span + i], (rows, WIDE)) > 0
        query = queries[target]
        grad = grads[target]
        held = keys[places_ref[base + 2 * span + i]]
        scores = contract_last(held, query) * FACTOR
        visible = apart <= places_ref[base + 3 * span + i]
        weights = jnp.where(visible, jnp.exp(scores - logsum_ref[target]), 0.0)
        dprobs = contract_last(held[:, :LATENT], grad)
        dscore = (weights * (dprobs - delta[target]) * FACTOR).astype(jnp.bfloat16)
        rounded = weights.astype(jnp.bfloat16)
        from_keys = contract_first(dscore, held)
        query_sums[0] += jnp.where(upper, from_keys, 0.0)
        query_sums[1] += jnp.where(upper, 0.0, from_keys)
        from_scores = jnp.dot(dscore, query, preferred_element_type=jnp.float32)
        from_values = jnp.dot(rounded, grad, preferred_element_type=jnp.float32)
        mine = pl.ds(i * SPAN, SPAN)
        from_scores = from_scores.reshape(SPAN, block, WIDE)
        from_values = from_values.reshape(SPAN, block, LATENT)
        slots[mine, :, :LATENT] += from_scores[:, :, :LATENT] + from_values
        slots[mine, :, LATENT:] += from_scores[:, :, LATENT:]
        return carry

    lax.fori_loop(0, tiles + 1, visit, 0)

    to_depth(0, step)

    @pl.when(step > 0)
    def _():
        to_depth(1, step - 1)

    for h in range(group):
        mine = slice(h * block, (h + 1) * block)
        cols = slice(h * NOPE_DIM, (h + 1) * NOPE_DIM)
        halves = [query_sums[late, mine, :], query_sums[early, mine, :]]
        grad_query = jnp.concatenate([x[:, :LATENT] for x in halves], axis=0)
        grad_query = grad_query.astype(jnp.bfloat16)
        d_nope_ref[:, cols] = jnp.dot(
            grad_query, key_up_ref[:, cols], preferred_element_type=jnp.float32
        ).astype(jnp.bfloat16)
        put_weight(1, h, contract_first(grad_query, nope_ref[:, cols]))
    start_weight(1, step)
    for t in range(2):
        held = slice(t * block, (t + 1) * block)
        source = late if t == 0 else early
        for h in range(0, group, 2):
            pair = [
                query_sums[source, k * block : (k + 1) * block, LATENT:][:, :ROPE_DIM]
                for k in (h, h + 1)
            ]
            d_rope_ref[held, h * ROPE_DIM : (h + 2) * ROPE_DIM] = jnp.concatenate(
                pair, axis=1
            ).astype(jnp.bfloat16)

    @pl.when(step == steps - 1)
    def _():
        def chosen(at):
            return jnp.broadcast_to(places_ref[at], (SPAN, block, WIDE)) > 0

        def combine(t, carry):
            here = pl.ds(t * SPAN, SPAN)
            there = pl.ds((tiles - 1 - t) * SPAN, SPAN)
            other = slots[there]
            above = chosen(base + 4 * span + t)
            lowest = chosen(base + 5 * span + t)
            slots[here] = (
                slots[here]
                + jnp.where(above, other, 0.0)
                + jnp.where(lowest, slots[tiles * SPAN :], 0.0)
            )
            slots[there] = jnp.where(above, 0.0, other)
            return carry

        lax.fori_loop(0, tiles // 2, combine, 0)

        for i in range(sides):

            def restore(j, carry):
                for c in range(2):
                    for half in range(2):
                        b = ((i * depth + j) * 2 + c) * 2 + half
                        k_part[i, j, c, half * block : (half + 1) * block, :] = slots[
                            places_ref[STORED + blocks + b]
                        ].astype(k_part.dtype)
                return carry

            lax.fori_loop(0, depth, restore, 0)

        def rows_of(target):
            return pl.ds(pl.multiple_of(target * share, share), share)

        keys_core = remote(k_part.at[:, :, 1 - core], k_recv1, "core", 1 - core, both(k1))
        keys_core.start()
        keys_core.wait_recv()
        for i in range(sides):
            for j in range(depth):
                total = wide(k_part[i, j, core]) + wide(k_recv1[i, j])
                k_recv1[i, j] = total.astype(k_recv1.dtype)
        keys_head = [
            remote(
                k_recv1.at[:, :, rows_of(partner("head", k)), :],
                k_recv2.at[k - 1],
                "head",
                partner("head", k),
                both(k2, k - 1),
            )
            for k in range(1, heads)
        ]
        for copy in keys_head:
            copy.start()
        to_side(1, step)
        for copy in keys_head:
            copy.wait_recv()
        for i in range(sides):
            for j in range(depth):
                total = wide(k_recv1[i, j, rows_of(head), :])
                for k in range(heads - 1):
                    total = total + wide(k_recv2[k, i, j])
                k_sum2[i, j] = total.astype(k_sum2.dtype)
        keys_side = [
            remote(
                k_sum2.at[partner("inner", k)],
                k_recv3.at[k - 1],
                "inner",
                partner("inner", k),
                both(k3, k - 1),
            )
            for k in range(1, sides)
        ]
        for copy in keys_side:
            copy.start()
        to_depth(1, step)
        for copy in keys_side:
            copy.wait_recv()
        for j in range(depth):
            total = wide(k_sum2[inner, j])
            for k in range(sides - 1):
                total = total + wide(k_recv3[k, j])
            k_sum3[j] = total.astype(k_sum3.dtype)
        keys_depth = [
            remote(
                k_sum3.at[partner("depth", k)],
                k_recv4.at[k - 1],
                "depth",
                partner("depth", k),
                both(k4, k - 1),
            )
            for k in range(1, depth)
        ]
        for copy in keys_depth:
            copy.start()

        def finish(g, carry):
            finish_weight(0, g, d_value_up_ref)
            finish_weight(1, g, d_key_up_ref)
            return carry

        lax.fori_loop(0, steps, finish, 0)
        for copy in keys_depth:
            copy.wait_recv()
        total = wide(k_sum3[level])
        for k in range(depth - 1):
            total = total + wide(k_recv4[k])
        k_own[rows_of(head), :] = total.astype(k_own.dtype)
        keys_last = [
            remote(
                k_own.at[rows_of(head), :],
                k_own.at[rows_of(head), :],
                "head",
                partner("head", k),
                both(k5, k - 1),
            )
            for k in range(1, heads)
        ]
        for copy in keys_last:
            copy.start()

        def drain(g, carry):
            finish_sends(0, g)
            finish_sends(1, g)
            return carry

        lax.fori_loop(0, steps, drain, 0)
        for k in range(1, depth):
            depth_key(k).wait_send()
        for j in range(depth):
            for k in range(1, sides):
                side_key(k, j).wait_send()
            for k in range(sides):
                core_key(k, j).wait_send()
        for copy in [keys_core] + keys_head + keys_side + keys_depth:
            copy.wait_send()
        for copy in keys_last:
            copy.wait()
        d_latent_ref[...] = k_own[:, :LATENT]
        d_key_rope_ref[...] = k_own[:, LATENT:][:, :ROPE_DIM]


def fused(
    sizes,
    group,
    places,
    own_keys,
    query_nope,
    query_rope,
    key_up,
    value_up,
    saved,
    upstream,
    logsum,
):
    depth, sides, heads = sizes["depth"], sizes["inner"], sizes["head"]
    owners = sides * depth * 2
    tokens = query_nope.shape[0]
    local_heads = query_nope.shape[1] // NOPE_DIM
    steps = local_heads // group
    block = tokens // 2
    length = owners * tokens
    blocks = length // block
    rows = group * block
    share = LATENT // owners
    totals = logsum.reshape(2, block, local_heads).transpose(0, 2, 1)
    totals = totals.reshape(2, 1, local_heads * block)
    whole = lambda i: (0, 0)
    part = lambda i: (0, i)
    narrow = lambda *shape: pltpu.VMEM(shape, jnp.bfloat16)
    full = lambda *shape: pltpu.VMEM(shape, jnp.float32)
    dma = lambda *shape: pltpu.SemaphoreType.DMA(shape)
    piece = (share, group * NOPE_DIM)
    mine = (tokens, WIDE)
    split = (tokens // heads, WIDE)
    pairs = length * local_heads * tokens // 2
    return pl.pallas_call(
        functools.partial(fused_kernel, sizes, group, block, blocks),
        grid=(steps,),
        in_specs=[
            pl.BlockSpec(memory_space=pltpu.SMEM),
            pl.BlockSpec(mine, whole),
            pl.BlockSpec((tokens, group * NOPE_DIM), part),
            pl.BlockSpec((tokens, group * ROPE_DIM), part),
            pl.BlockSpec((LATENT, group * NOPE_DIM), part),
            pl.BlockSpec((LATENT, group * VALUE_DIM), part),
            pl.BlockSpec((tokens, group * LATENT), part),
            pl.BlockSpec((tokens, group * VALUE_DIM), part),
            pl.BlockSpec((2, 1, rows), lambda i: (0, 0, i)),
        ],
        out_specs=[
            pl.BlockSpec((tokens, group * NOPE_DIM), part),
            pl.BlockSpec((tokens, group * ROPE_DIM), part),
            pl.BlockSpec((tokens, LATENT), whole),
            pl.BlockSpec((tokens, ROPE_DIM), whole),
            pl.BlockSpec((share, local_heads * NOPE_DIM), whole),
            pl.BlockSpec((share, local_heads * VALUE_DIM), whole),
        ],
        scratch_shapes=[
            narrow(blocks, block, WIDE),
            narrow(blocks // SPAN, SPAN * block, WIDE),
            full(blocks + SPAN, block, WIDE),
            narrow(2, rows, WIDE),
            narrow(2, rows, LATENT),
            full(2, 1, rows),
            full(2, rows, WIDE),
            narrow(2, steps, sides, depth, 2, *piece),
            narrow(2, steps, sides, depth, *piece),
            narrow(2, steps, sides - 1, depth, *piece),
            narrow(2, steps, depth, *piece),
            narrow(2, steps, depth - 1, *piece),
            narrow(sides, depth, 2, *mine),
            narrow(sides, depth, *mine),
            narrow(heads - 1, sides, depth, *split),
            narrow(sides, depth, *split),
            narrow(sides - 1, depth, *split),
            narrow(depth, *split),
            narrow(depth - 1, *split),
            narrow(*mine),
            dma(2, depth - 1),
            dma(2, sides - 1, depth),
            dma(2, sides, depth),
            dma(2, 2, steps),
            dma(2, 2, steps, sides - 1),
            dma(2, 2, steps, depth - 1),
            dma(2),
            dma(2, heads - 1),
            dma(2, sides - 1),
            dma(2, depth - 1),
            dma(2, heads - 1),
        ],
        out_shape=[
            jax.ShapeDtypeStruct(query_nope.shape, jnp.bfloat16),
            jax.ShapeDtypeStruct(query_rope.shape, jnp.bfloat16),
            jax.ShapeDtypeStruct((tokens, LATENT), jnp.bfloat16),
            jax.ShapeDtypeStruct((tokens, ROPE_DIM), jnp.bfloat16),
            jax.ShapeDtypeStruct((share, local_heads * NOPE_DIM), jnp.float32),
            jax.ShapeDtypeStruct((share, local_heads * VALUE_DIM), jnp.float32),
        ],
        compiler_params=pltpu.CompilerParams(
            collective_id=0, has_side_effects=True, vmem_limit_bytes=VMEM
        ),
        cost_estimate=pl.CostEstimate(
            flops=pairs * 2 * 2752, bytes_accessed=20 * 1024 * 1024, transcendentals=pairs
        ),
        name="latent_attention_backward",
    )(places, own_keys, query_nope, query_rope, key_up, value_up, saved, upstream, totals)


def local(
    query_nope,
    query_rope,
    latent,
    key_rope,
    key_up,
    value_up,
    latent_out,
    out_grad,
    logsum,
    block_order,
):
    axes = ("inner", "outer")
    heads = query_nope.shape[1] // NOPE_DIM
    blocks = block_order.shape[0]
    group = min(8, heads)
    sizes = {
        "head": lax.axis_size("head"),
        "inner": lax.axis_size("inner"),
        "depth": lax.axis_size("outer") // 2,
        "core": 2,
    }
    own_keys = jnp.concatenate([latent, key_rope, jnp.zeros_like(key_rope)], axis=1)
    index = lax.iota(jnp.int32, blocks)
    held = (block_order[:, None] == index[None, :]).astype(jnp.int32)
    stored = jnp.sum(held * index[:, None], axis=0)
    own = lax.dynamic_slice_in_dim(block_order, 2 * lax.axis_index(axes), 2, 0)
    tiles = blocks // SPAN
    late = (own[1] > own[0]).astype(jnp.int32)
    later, earlier = jnp.max(own), jnp.min(own)
    top, low = later // SPAN, earlier // SPAN
    slot = lax.iota(jnp.int32, tiles + 1)
    upper = (slot <= jnp.minimum(top, tiles - 1)).astype(jnp.int32)
    lower_tile = jnp.where(slot == tiles, low, tiles - 1 - slot)
    tile_of = jnp.where(upper > 0, slot, lower_tile)
    limit = jnp.where(upper > 0, later, earlier) - tile_of * SPAN
    places = jnp.concatenate(
        [
            jnp.stack([late, 1 - late]),
            stored,
            block_order,
            jnp.where(upper > 0, late, 1 - late),
            upper,
            tile_of,
            limit * (query_nope.shape[0] // 2),
            (tiles - 1 - slot > top).astype(jnp.int32),
            (slot == low).astype(jnp.int32),
        ]
    )
    return fused(
        sizes,
        group,
        places,
        own_keys,
        query_nope,
        query_rope,
        key_up,
        value_up,
        latent_out,
        out_grad,
        logsum,
    )


def solution(mesh):
    placed = (
        P(("inner", "outer"), "head"),
        P(("inner", "outer"), "head"),
        P(("inner", "outer"), None),
        P(("inner", "outer"), None),
        P(None, "head"),
        P(None, "head"),
        P(("inner", "outer"), "head"),
        P(("inner", "outer"), "head"),
        P(("inner", "outer"), "head"),
        P(),
    )
    return jax.shard_map(
        local,
        mesh=mesh,
        in_specs=placed,
        out_specs=(
            P(("inner", "outer"), "head"),
            P(("inner", "outer"), "head"),
            P(("inner", "outer"), None),
            P(("inner", "outer"), None),
            P(("inner", "outer"), "head"),
            P(("inner", "outer"), "head"),
        ),
        check_vma=False,
    )
```

time: 364 us -> 161 us (0.44)
  waiting for transfers between devices: 242 us -> 0 us
  Pallas kernels: 68.2 us -> 135 us
  blocking collectives: 28.2 us -> 0 us
  local copies, waits for them, and re-layouts: 6.08 us -> 14.2 us
  between operations: 13.8 us -> 7.21 us
    reduce_scatter x3 -> x0, waiting for transfers between devices: 205 us -> none  [the longest x1 74.8 us: local(): lax.psum_scatter(value_weight, axes, scatter_dimension=0, tiled=True)]
    pallas_call x2 -> x1, Pallas kernels: 68.2 us -> 135 us  [fused(): pl.pallas_call(functools.partial(fused_kernel, sizes, group, block, block...]
    all_gather x1 -> x0, blocking collectives: 28.2 us -> none  [local(): all_rope = lax.all_gather(key_rope, axes, axis=0, tiled=True)]
    psum x1 -> x0, waiting for transfers between devices: 21.4 us -> none  [local(): own_keys = lax.psum(own_keys, 'head')]
    all_gather x1 -> x0, waiting for transfers between devices: 14.3 us -> none  [local(): all_keys = lax.all_gather(latent, axes, axis=0, tiled=True)]
    unnamed x2 -> x8, local copies, waits for them, and re-layouts: 1.52 us -> 9.22 us
  transfers between devices with their start and end apart: 5 -> 0, of which waited for: 5 -> 0; matrix products, arithmetic and copies ran while one was open for 3% -> 0% of each run, Pallas kernels for 2% -> 0%
where the time goes in v3:
time: 161 us
  Pallas kernels  135 us (84%)
  local copies, waits for them, and re-layouts  14.2 us (9%)
  between operations  7.21 us (4%)
  other arithmetic  5.03 us (3%)
    pallas_call x1, Pallas kernels, fused(): pl.pallas_call(functools.partial(fused_kernel, sizes, group, block, block...  135 us
    unnamed x8, local copies, waits for them, and re-layouts  9.22 us

profile of v3, /device:TPU:0, one launch (start us, length us, event | category | flops | bytes accessed | tf_op | source)
XLA Modules:
  0.0 160.9 jit_solution(4383291352216932687)
XLA Ops:
  0.6 0.7 select_reduce_fusion
  1.4 1.4 fusion.1
  8.0 0.6 fusion.2
  9.9 1.3 fusion
  11.2 1.3 concatenate.6.places_ref
  12.5 0.1 pad.2.clone
  12.5 0.8 copy.19
  13.4 0.8 reshape.22
  14.2 0.7 reshape.23.logsum_ref
  14.9 1.6 maximum_maximum_fusion.own_ref
  16.5 134.5 %latent_attention_backward.1 = (bf16[128,4096]{1,0:T(8,128)(2,1)}, bf16[128,2048]{1,0:T(8,128)(2,1)}, bf16[128,512]{1,0:T(8,128)(2,1)}, bf16[128,64]{1,0:T(8,128...) custom-call(s32[120]{0:T(128)} %concatenate.6.places_ref, bf16[128,640]{1,0:T(8,128)(2,1)} %maximum_maximum_fusion.own_ref, ...), custom_call_target="tpu_custom_call" | custom-call | flops 23085449216 | bytes 20971520 | tf_op jit(solution)/shard_map/latent_attention_backward/pallas_call | solution.py:557
  151.0 0.0 copy-start
  151.0 1.5 copy.21
  152.5 2.3 %copy.29 = bf16[128,4096]{1,0:T(8,128)(2,1)} copy(bf16[128,4096]{1,0:T(8,128)(2,1)} %get-tuple-element.33) | data formatting | bytes 2097152
  154.8 1.9 %copy.30 = bf16[128,2048]{1,0:T(8,128)(2,1)} copy(bf16[128,2048]{1,0:T(8,128)(2,1)} %get-tuple-element.34) | data formatting | bytes 1048576
  156.7 1.6 copy.31
  158.2 1.9 %copy.32 = f32[32,4096]{1,0:T(8,128)} copy(f32[32,4096]{1,0:T(8,128)} %get-tuple-element.37) | data formatting | bytes 1048576
  160.1 0.0 copy-done
  160.1 0.8 copy.33
  (5 shorter events, 0.0 us)
Async XLA Ops:
  151.0 9.1 %copy-start = (f32[32,4096]{1,0:T(8,128)S(1)}, f32[32,4096]{1,0:T(8,128)}, u32[]{:S(2)}) copy-start(f32[32,4096]{1,0:T(8,128)} %get-tuple-element.38) | copy-start | bytes 1572868

commit v4 on v3

--- a/solution.py
+++ b/solution.py
@@ -2,6 +2,7 @@
 
 import jax
 import jax.numpy as jnp
+import numpy as np
 from jax import lax
 from jax.experimental import pallas as pl
 from jax.experimental.pallas import tpu as pltpu
@@ -12,8 +13,9 @@
 NOPE_DIM = 128
 VALUE_DIM = 128
 WIDE = 640
+PIECE = 128
 SPAN = 4
-STORED = 2
+FIELDS = 7
 FACTOR = float(NOPE_DIM + ROPE_DIM) ** (-0.5)
 VMEM = 60 * 1024 * 1024
 
@@ -72,8 +74,11 @@
     group,
     block,
     blocks,
-    places_ref,
-    own_ref,
+    stored_ref,
+    order_ref,
+    table_ref,
+    own_lat_ref,
+    own_rope_ref,
     nope_ref,
     rope_ref,
     key_up_ref,
@@ -127,6 +132,8 @@
     tiles = blocks // SPAN
     width = group * NOPE_DIM
     share = 2 * block // heads
+    span = tiles + 1
+    me = (inner * depth + level) * 2 + core
     step = pl.program_id(0)
     steps = pl.num_programs(0)
 
@@ -238,7 +245,12 @@
     @pl.when(step == 0)
     def _():
         greet(place, spot, sizes, ("core", "depth", "inner", "head"))
-        gathered[owned(inner, level, core)] = own_ref[...].reshape(2, block, WIDE)
+        part = own_rope_ref[...]
+        mine = owned(inner, level, core)
+        gathered[mine, :, :LATENT] = own_lat_ref[...].reshape(2, block, LATENT)
+        gathered[mine, :, LATENT:] = jnp.concatenate([part, jnp.zeros_like(part)], axis=1).reshape(
+            2, block, WIDE - LATENT
+        )
         for k in range(1, depth):
             depth_key(k).start()
         for k in range(1, sides):
@@ -305,7 +317,7 @@
         def sort(p, carry):
             for k in range(SPAN):
                 keys[p, k * block : (k + 1) * block, :] = gathered[
-                    places_ref[STORED + p * SPAN + k]
+                    stored_ref[p * SPAN + k]
                 ]
             return carry
 
@@ -313,29 +325,30 @@
 
     to_side(0, step)
 
-    span = tiles + 1
-    base = STORED + 2 * blocks
-    late = places_ref[0]
-    early = places_ref[1]
+    late = table_ref[me, 6 * span]
+    early = table_ref[me, 6 * span + 1]
     key_index = lax.broadcasted_iota(jnp.int32, (tile, rows), 0)
     row_index = lax.rem(lax.broadcasted_iota(jnp.int32, (tile, rows), 1), block)
     apart = key_index - row_index
 
-    def visit(i, carry):
-        target = places_ref[base + i]
-        upper = jnp.broadcast_to(places_ref[base + span + i], (rows, WIDE)) > 0
+    def visit(shared, i, carry):
+        target = table_ref[me, i]
         query = queries[target]
         grad = grads[target]
-        held = keys[places_ref[base + 2 * span + i]]
+        held = keys[table_ref[me, 2 * span + i]]
         scores = contract_last(held, query) * FACTOR
-        visible = apart <= places_ref[base + 3 * span + i]
+        visible = apart <= table_ref[me, 3 * span + i]
         weights = jnp.where(visible, jnp.exp(scores - logsum_ref[target]), 0.0)
         dprobs = contract_last(held[:, :LATENT], grad)
         dscore = (weights * (dprobs - delta[target]) * FACTOR).astype(jnp.bfloat16)
         rounded = weights.astype(jnp.bfloat16)
         from_keys = contract_first(dscore, held)
-        query_sums[0] += jnp.where(upper, from_keys, 0.0)
-        query_sums[1] += jnp.where(upper, 0.0, from_keys)
+        if shared:
+            upper = jnp.broadcast_to(table_ref[me, span + i], (rows, WIDE)) > 0
+            query_sums[0] += jnp.where(upper, from_keys, 0.0)
+            query_sums[1] += jnp.where(upper, 0.0, from_keys)
+        else:
+            query_sums[0] += from_keys
         from_scores = jnp.dot(dscore, query, preferred_element_type=jnp.float32)
         from_values = jnp.dot(rounded, grad, preferred_element_type=jnp.float32)
         mine = pl.ds(i * SPAN, SPAN)
@@ -345,7 +358,8 @@
         slots[mine, :, LATENT:] += from_scores[:, :, LATENT:]
         return carry
 
-    lax.fori_loop(0, tiles + 1, visit, 0)
+    lax.fori_loop(0, tiles // 2, functools.partial(visit, False), 0)
+    lax.fori_loop(tiles // 2, tiles + 1, functools.partial(visit, True), 0)
 
     to_depth(0, step)
 
@@ -379,14 +393,14 @@
     @pl.when(step == steps - 1)
     def _():
         def chosen(at):
-            return jnp.broadcast_to(places_ref[at], (SPAN, block, WIDE)) > 0
+            return jnp.broadcast_to(table_ref[me, at], (SPAN, block, WIDE)) > 0
 
         def combine(t, carry):
             here = pl.ds(t * SPAN, SPAN)
             there = pl.ds((tiles - 1 - t) * SPAN, SPAN)
             other = slots[there]
-            above = chosen(base + 4 * span + t)
-            lowest = chosen(base + 5 * span + t)
+            above = chosen(4 * span + t)
+            lowest = chosen(5 * span + t)
             slots[here] = (
                 slots[here]
                 + jnp.where(above, other, 0.0)
@@ -404,7 +418,7 @@
                     for half in range(2):
                         b = ((i * depth + j) * 2 + c) * 2 + half
                         k_part[i, j, c, half * block : (half + 1) * block, :] = slots[
-                            places_ref[STORED + blocks + b]
+                            order_ref[b]
                         ].astype(k_part.dtype)
                 return carry
 
@@ -413,66 +427,94 @@
         def rows_of(target):
             return pl.ds(pl.multiple_of(target * share, share), share)
 
-        keys_core = remote(k_part.at[:, :, 1 - core], k_recv1, "core", 1 - core, both(k1))
-        keys_core.start()
-        keys_core.wait_recv()
-        for i in range(sides):
+        pieces = WIDE // PIECE
+        cols = [slice(c * PIECE, (c + 1) * PIECE) for c in range(pieces)]
+        keys_core = [
+            remote(
+                k_part.at[:, :, 1 - core, :, cols[c]],
+                k_recv1.at[c],
+                "core",
+                1 - core,
+                both(k1, c),
+            )
+            for c in range(pieces)
+        ]
+        for copy in keys_core:
+            copy.start()
+        keys_head, keys_side, keys_depth = [], [], []
+        for c in range(pieces):
+            keys_core[c].wait_recv()
+            for i in range(sides):
+                for j in range(depth):
+                    total = wide(k_part[i, j, core, :, cols[c]]) + wide(k_recv1[c, i, j])
+                    k_recv1[c, i, j] = total.astype(k_recv1.dtype)
+            copies = [
+                remote(
+                    k_recv1.at[c, :, :, rows_of(partner("head", k)), :],
+                    k_recv2.at[c, k - 1],
+                    "head",
+                    partner("head", k),
+                    both(k2, c, k - 1),
+                )
+                for k in range(1, heads)
+            ]
+            for copy in copies:
+                copy.start()
+            keys_head.append(copies)
+        to_side(1, step)
+
+        def head_to_side(c):
+            for copy in keys_head[c]:
+                copy.wait_recv()
+            for i in range(sides):
+                for j in range(depth):
+                    total = wide(k_recv1[c, i, j, rows_of(head), :])
+                    for k in range(heads - 1):
+                        total = total + wide(k_recv2[c, k, i, j])
+                    k_sum2[c, i, j] = total.astype(k_sum2.dtype)
+            copies = [
+                remote(
+                    k_sum2.at[c, partner("inner", k)],
+                    k_recv3.at[c, k - 1],
+                    "inner",
+                    partner("inner", k),
+                    both(k3, c, k - 1),
+                )
+                for k in range(1, sides)
+            ]
+            for copy in copies:
+                copy.start()
+            keys_side.append(copies)
+
+        def side_to_depth(c):
+            for copy in keys_side[c]:
+                copy.wait_recv()
             for j in range(depth):
-                total = wide(k_part[i, j, core]) + wide(k_recv1[i, j])
-                k_recv1[i, j] = total.astype(k_recv1.dtype)
-        keys_head = [
-            remote(
-                k_recv1.at[:, :, rows_of(partner("head", k)), :],
-                k_recv2.at[k - 1],
-                "head",
-                partner("head", k),
-                both(k2, k - 1),
-            )
-            for k in range(1, heads)
-        ]
-        for copy in keys_head:
-            copy.start()
-        to_side(1, step)
-        for copy in keys_head:
-            copy.wait_recv()
-        for i in range(sides):
-            for j in range(depth):
-                total = wide(k_recv1[i, j, rows_of(head), :])
-                for k in range(heads - 1):
-                    total = total + wide(k_recv2[k, i, j])
-                k_sum2[i, j] = total.astype(k_sum2.dtype)
-        keys_side = [
-            remote(
-                k_sum2.at[partner("inner", k)],
-                k_recv3.at[k - 1],
-                "inner",
-                partner("inner", k),
-                both(k3, k - 1),
-            )
-            for k in range(1, sides)
-        ]
-        for copy in keys_side:
-            copy.start()
-        to_depth(1, step)
-        for copy in keys_side:
-            copy.wait_recv()
-        for j in range(depth):
-            total = wide(k_sum2[inner, j])
-            for k in range(sides - 1):
-                total = total + wide(k_recv3[k, j])
-            k_sum3[j] = total.astype(k_sum3.dtype)
-        keys_depth = [
-            remote(
-                k_sum3.at[partner("depth", k)],
-                k_recv4.at[k - 1],
-                "depth",
-                partner("depth", k),
-                both(k4, k - 1),
-            )
-            for k in range(1, depth)
-        ]
-        for copy in keys_depth:
-            copy.start()
+                total = wide(k_sum2[c, inner, j])
+                for k in range(sides - 1):
+                    total = total + wide(k_recv3[c, k, j])
+                k_sum3[c, j] = total.astype(k_sum3.dtype)
+            copies = [
+                remote(
+                    k_sum3.at[c, partner("depth", k)],
+                    k_recv4.at[c, k - 1],
+                    "depth",
+                    partner("depth", k),
+                    both(k4, c, k - 1),
+                )
+                for k in range(1, depth)
+            ]
+            for copy in copies:
+                copy.start()
+            keys_depth.append(copies)
+
+        for c in range(pieces):
+            head_to_side(c)
+            if c == 1:
+                to_depth(1, step)
+            if c > 0:
+                side_to_depth(c - 1)
+        side_to_depth(pieces - 1)
 
         def finish(g, carry):
             finish_weight(0, g, d_value_up_ref)
@@ -480,12 +522,13 @@
             return carry
 
         lax.fori_loop(0, steps, finish, 0)
-        for copy in keys_depth:
-            copy.wait_recv()
-        total = wide(k_sum3[level])
-        for k in range(depth - 1):
-            total = total + wide(k_recv4[k])
-        k_own[rows_of(head), :] = total.astype(k_own.dtype)
+        for c in range(pieces):
+            for copy in keys_depth[c]:
+                copy.wait_recv()
+            total = wide(k_sum3[c, level])
+            for k in range(depth - 1):
+                total = total + wide(k_recv4[c, k])
+            k_own[rows_of(head), cols[c]] = total.astype(k_own.dtype)
         keys_last = [
             remote(
                 k_own.at[rows_of(head), :],
@@ -512,7 +555,7 @@
                 side_key(k, j).wait_send()
             for k in range(sides):
                 core_key(k, j).wait_send()
-        for copy in [keys_core] + keys_head + keys_side + keys_depth:
+        for copy in keys_core + sum(keys_head + keys_side + keys_depth, []):
             copy.wait_send()
         for copy in keys_last:
             copy.wait()
@@ -523,8 +566,11 @@
 def fused(
     sizes,
     group,
-    places,
-    own_keys,
+    stored,
+    order,
+    table,
+    latent,
+    key_rope,
     query_nope,
     query_rope,
     key_up,
@@ -552,14 +598,18 @@
     dma = lambda *shape: pltpu.SemaphoreType.DMA(shape)
     piece = (share, group * NOPE_DIM)
     mine = (tokens, WIDE)
-    split = (tokens // heads, WIDE)
+    split = (tokens // heads, PIECE)
+    pieces = WIDE // PIECE
     pairs = length * local_heads * tokens // 2
-    return pl.pallas_call(
+    results = pl.pallas_call(
         functools.partial(fused_kernel, sizes, group, block, blocks),
         grid=(steps,),
         in_specs=[
             pl.BlockSpec(memory_space=pltpu.SMEM),
-            pl.BlockSpec(mine, whole),
+            pl.BlockSpec(memory_space=pltpu.SMEM),
+            pl.BlockSpec(memory_space=pltpu.SMEM),
+            pl.BlockSpec((tokens, LATENT), whole),
+            pl.BlockSpec((tokens, ROPE_DIM), whole),
             pl.BlockSpec((tokens, group * NOPE_DIM), part),
             pl.BlockSpec((tokens, group * ROPE_DIM), part),
             pl.BlockSpec((LATENT, group * NOPE_DIM), part),
@@ -590,12 +640,12 @@
             narrow(2, steps, depth, *piece),
             narrow(2, steps, depth - 1, *piece),
             narrow(sides, depth, 2, *mine),
-            narrow(sides, depth, *mine),
-            narrow(heads - 1, sides, depth, *split),
-            narrow(sides, depth, *split),
-            narrow(sides - 1, depth, *split),
-            narrow(depth, *split),
-            narrow(depth - 1, *split),
+            narrow(pieces, sides, depth, tokens, PIECE),
+            narrow(pieces, heads - 1, sides, depth, *split),
+            narrow(pieces, sides, depth, *split),
+            narrow(pieces, sides - 1, depth, *split),
+            narrow(pieces, depth, *split),
+            narrow(pieces, depth - 1, *split),
             narrow(*mine),
             dma(2, depth - 1),
             dma(2, sides - 1, depth),
@@ -603,10 +653,10 @@
             dma(2, 2, steps),
             dma(2, 2, steps, sides - 1),
             dma(2, 2, steps, depth - 1),
-            dma(2),
-            dma(2, heads - 1),
-            dma(2, sides - 1),
-            dma(2, depth - 1),
+            dma(2, pieces),
+            dma(2, pieces, heads - 1),
+            dma(2, pieces, sides - 1),
+            dma(2, pieces, depth - 1),
             dma(2, heads - 1),
         ],
         out_shape=[
@@ -624,7 +674,44 @@
             flops=pairs * 2 * 2752, bytes_accessed=20 * 1024 * 1024, transcendentals=pairs
         ),
         name="latent_attention_backward",
-    )(places, own_keys, query_nope, query_rope, key_up, value_up, saved, upstream, totals)
+    )(
+        stored,
+        order,
+        table,
+        latent,
+        key_rope,
+        query_nope,
+        query_rope,
+        key_up,
+        value_up,
+        saved,
+        upstream,
+        totals,
+    )
+    return hand_over(results)
+
+
+def hand_over_kernel(count, *refs):
+    sems = refs[-1]
+    copies = [
+        pltpu.make_async_copy(refs[i], refs[count + i], sems.at[i]) for i in range(count)
+    ]
+    for copy in copies:
+        copy.start()
+    for copy in copies:
+        copy.wait()
+
+
+def hand_over(arrays):
+    count = len(arrays)
+    return pl.pallas_call(
+        functools.partial(hand_over_kernel, count),
+        in_specs=[pl.BlockSpec(memory_space=pl.ANY)] * count,
+        out_specs=[pl.BlockSpec(memory_space=pl.ANY)] * count,
+        out_shape=[jax.ShapeDtypeStruct(x.shape, x.dtype) for x in arrays],
+        scratch_shapes=[pltpu.SemaphoreType.DMA((count,))],
+        name="hand_over",
+    )(*arrays)
 
 
 def local(
@@ -649,38 +736,37 @@
         "depth": lax.axis_size("outer") // 2,
         "core": 2,
     }
-    own_keys = jnp.concatenate([latent, key_rope, jnp.zeros_like(key_rope)], axis=1)
     index = lax.iota(jnp.int32, blocks)
     held = (block_order[:, None] == index[None, :]).astype(jnp.int32)
     stored = jnp.sum(held * index[:, None], axis=0)
-    own = lax.dynamic_slice_in_dim(block_order, 2 * lax.axis_index(axes), 2, 0)
     tiles = blocks // SPAN
-    late = (own[1] > own[0]).astype(jnp.int32)
-    later, earlier = jnp.max(own), jnp.min(own)
+    span = tiles + 1
+    pair = block_order.reshape(-1, 2)
+    first, second = pair[:, :1], pair[:, 1:]
+    late = (second > first).astype(jnp.int32)
+    later, earlier = jnp.maximum(first, second), jnp.minimum(first, second)
     top, low = later // SPAN, earlier // SPAN
-    slot = lax.iota(jnp.int32, tiles + 1)
-    upper = (slot <= jnp.minimum(top, tiles - 1)).astype(jnp.int32)
-    lower_tile = jnp.where(slot == tiles, low, tiles - 1 - slot)
-    tile_of = jnp.where(upper > 0, slot, lower_tile)
-    limit = jnp.where(upper > 0, later, earlier) - tile_of * SPAN
-    places = jnp.concatenate(
-        [
-            jnp.stack([late, 1 - late]),
-            stored,
-            block_order,
-            jnp.where(upper > 0, late, 1 - late),
-            upper,
-            tile_of,
-            limit * (query_nope.shape[0] // 2),
-            (tiles - 1 - slot > top).astype(jnp.int32),
-            (slot == low).astype(jnp.int32),
-        ]
-    )
+    column = np.arange(FIELDS * span, dtype=np.int32)[None, :]
+    field, slot = column // span, column % span
+    upper = slot <= jnp.minimum(top, tiles - 1)
+    tile_of = jnp.where(upper, slot, jnp.where(slot == tiles, low, tiles - 1 - slot))
+    limit = (jnp.where(upper, later, earlier) - tile_of * SPAN) * (query_nope.shape[0] // 2)
+    above = (tiles - 1 - slot > top).astype(jnp.int32)
+    table = jnp.where(slot == 0, late, 1 - late)
+    table = jnp.where(field == 5, (slot == low).astype(jnp.int32), table)
+    table = jnp.where(field == 4, above, table)
+    table = jnp.where(field == 3, limit, table)
+    table = jnp.where(field == 2, tile_of, table)
+    table = jnp.where(field == 1, upper.astype(jnp.int32), table)
+    table = jnp.where(field == 0, jnp.where(upper, late, 1 - late), table)
     return fused(
         sizes,
         group,
-        places,
-        own_keys,
+        stored,
+        block_order,
+        table,
+        latent,
+        key_rope,
         query_nope,
         query_rope,
         key_up,

time: 161 us -> 220 us (1.37)
  Pallas kernels: 135 us -> 211 us
  local copies, waits for them, and re-layouts: 14.2 us -> 5.11 us
  between operations: 7.21 us -> 0.66 us
    pallas_call x0 -> x1, Pallas kernels: none -> 85.5 us  [hand_over(): pl.pallas_call(functools.partial(hand_over_kernel, count), in_specs=[pl.B...]
    pallas_call x1, Pallas kernels: 135 us -> 125 us  [fused(): pl.pallas_call(functools.partial(fused_kernel, sizes, group, block, block...]
    unnamed x8 -> x1, local copies, waits for them, and re-layouts: 9.22 us -> 1.43 us
where the time goes in v4:
time: 220 us; the launch traced here: 219 us
  Pallas kernels  211 us (96%)
  local copies, waits for them, and re-layouts  5.11 us (2%)
  other arithmetic  3.12 us (1%)
    pallas_call x1, Pallas kernels, fused(): pl.pallas_call(functools.partial(fused_kernel, sizes, group, block, block...  125 us
    pallas_call x1, Pallas kernels, hand_over(): pl.pallas_call(functools.partial(hand_over_kernel, count), in_specs=[pl.B...  85.5 us

profile of v4, /device:TPU:0, one launch (start us, length us, event | category | flops | bytes accessed | tf_op | source)
XLA Modules:
  0.0 219.5 jit_solution(11858165657848559104)
XLA Ops:
  0.6 1.3 select_reduce_fusion.stored_ref
  1.9 0.7 reshape.22
  2.6 0.3 convert_reduce_fusion
  2.9 0.1 minimum_reduce_fusion
  3.0 1.5 fusion.4.table_ref
  4.5 1.4 copy.34.own_rope_ref
  5.9 0.8 reshape.23
  6.7 0.7 reshape.24.logsum_ref
  7.4 125.0 %latent_attention_backward.1 = (bf16[128,4096]{1,0:T(8,128)(2,1)}, bf16[128,2048]{1,0:T(8,128)(2,1)}, bf16[128,512]{1,0:T(8,128)(2,1)}, bf16[128,64]{1,0:T(8,128...) custom-call(s32[32]{0:T(128)} %select_reduce_fusion.stored_ref, s32[32]{0:T(128)} %order_ref.1, ...), custom_call_target="tpu_custom_call" | custom-call | flops 23085449216 | bytes 20971520 | tf_op jit(solution)/shard_map/latent_attention_backward/pallas_call | solution.py:604
  132.5 85.5 %hand_over.1 = (bf16[128,4096]{1,0:T(8,128)(2,1)}, bf16[128,2048]{1,0:T(8,128)(2,1)}, bf16[128,512]{1,0:T(8,128)(2,1)}, bf16[128,64]{1,0:T(8,128)(2,1)}, f32[32,4096]{1,0:T(8,128)}, /*index=5*/f32[32,4096]{1,0:T(8,128)}) custom-call(bf16[128,4096]{1,0:T(8,128)(2,1)} %get-tuple-element.12.refs_0_, bf16[128,2048]{1,0:T(8,128)(2,1)} %get-tuple-element.13.refs_1_, ...), custom_call_target="tpu_custom_call" | custom-call | tf_op jit(solution)/shard_map/hand_over/pallas_call | solution.py:707
  218.0 1.4 copy.35
  (1 shorter events, 0.0 us)

commit v5 on v4

--- a/solution.py
+++ b/solution.py
@@ -692,24 +692,18 @@
 
 
 def hand_over_kernel(count, *refs):
-    sems = refs[-1]
-    copies = [
-        pltpu.make_async_copy(refs[i], refs[count + i], sems.at[i]) for i in range(count)
-    ]
-    for copy in copies:
-        copy.start()
-    for copy in copies:
-        copy.wait()
+    for i in range(count):
+        refs[count + i][...] = refs[i][...]
 
 
 def hand_over(arrays):
     count = len(arrays)
     return pl.pallas_call(
         functools.partial(hand_over_kernel, count),
-        in_specs=[pl.BlockSpec(memory_space=pl.ANY)] * count,
-        out_specs=[pl.BlockSpec(memory_space=pl.ANY)] * count,
+        in_specs=[pl.BlockSpec(memory_space=pltpu.VMEM)] * count,
+        out_specs=[pl.BlockSpec(memory_space=pltpu.VMEM)] * count,
         out_shape=[jax.ShapeDtypeStruct(x.shape, x.dtype) for x in arrays],
-        scratch_shapes=[pltpu.SemaphoreType.DMA((count,))],
+        compiler_params=pltpu.CompilerParams(vmem_limit_bytes=VMEM),
         name="hand_over",
     )(*arrays)
 

time: 220 us -> 138 us (0.63)
  Pallas kernels: 211 us -> 128 us
    pallas_call x1, Pallas kernels: 85.5 us -> 3.31 us  [hand_over(): pl.pallas_call(functools.partial(hand_over_kernel, count), in_specs=[pl.B...]
where the time goes in v5:
time: 138 us; the launch traced here: 137 us
  Pallas kernels  128 us (93%)
  local copies, waits for them, and re-layouts  5.11 us (4%)
  other arithmetic  3.12 us (2%)
    pallas_call x1, Pallas kernels, fused(): pl.pallas_call(functools.partial(fused_kernel, sizes, group, block, block...  125 us
    pallas_call x1, Pallas kernels, hand_over(): pl.pallas_call(functools.partial(hand_over_kernel, count), in_specs=[pl.B...  3.31 us

profile of v5, /device:TPU:0, one launch (start us, length us, event | category | flops | bytes accessed | tf_op | source)
XLA Modules:
  0.0 137.3 jit_solution(17081364936710358405)
XLA Ops:
  0.6 1.3 select_reduce_fusion.stored_ref
  1.9 0.7 reshape.22
  2.6 0.3 convert_reduce_fusion
  2.9 0.1 minimum_reduce_fusion
  3.0 1.5 %fusion.4.table_ref = s32[16,63]{1,0:T(8,128)} fusion(s32[16]{0:T(128)S(1)} %get-tuple-element.46, s32[16]{0:T(128)S(1)} %get-tuple-element.45, s32[63]{0:T(128)} %constant.67, s32[16]{0:T(128)S(1)} %get-tuple-element.42, s32[16]{0:T(128)S(1)} %get-tuple-element.41, s32[63]{0:T(128)} %constant.63, s32[16]{0:T(128)S(1)} %get-tuple-element.37, ...), kind=kLoop, calls=%fused_computation.21 | loop fusion | flops 20160 | bytes 5488 | tf_op jit(solution)/shard_map/jit(_where)/select_n | solution.py:755
  4.5 1.4 %copy.34.own_rope_ref = bf16[128,64]{1,0:T(8,128)(2,1)} copy(bf16[128,64]{0,1:T(8,128)(2,1)} %param.24) | data formatting | bytes 32768 | tf_op args[3]
  5.9 0.8 reshape.23
  6.7 0.7 reshape.24.logsum_ref
  7.4 125.1 %latent_attention_backward.1 = (bf16[128,4096]{1,0:T(8,128)(2,1)}, bf16[128,2048]{1,0:T(8,128)(2,1)}, bf16[128,512]{1,0:T(8,128)(2,1)}, bf16[128,64]{1,0:T(8,128...) custom-call(s32[32]{0:T(128)} %select_reduce_fusion.stored_ref, s32[32]{0:T(128)} %order_ref.1, ...), custom_call_target="tpu_custom_call" | custom-call | flops 23085449216 | bytes 20971520 | tf_op jit(solution)/shard_map/latent_attention_backward/pallas_call | solution.py:604
  132.5 3.3 %hand_over.1 = (bf16[128,4096]{1,0:T(8,128)(2,1)}, bf16[128,2048]{1,0:T(8,128)(2,1)}, bf16[128,512]{1,0:T(8,128)(2,1)}, bf16[128,64]{1,0:T(8,128)(2,1)}, f32[32,4096]{1,0:T(8,128)}, /*index=5*/f32[32,4096]{1,0:T(8,128)}) custom-call(bf16[128,4096]{1,0:T(8,128)(2,1)} %get-tuple-element.12.refs_0_, bf16[128,2048]{1,0:T(8,128)(2,1)} %get-tuple-element.13.refs_1_, ...), custom_call_target="tpu_custom_call" | custom-call | tf_op jit(solution)/shard_map/hand_over/pallas_call | solution.py:701
  135.8 1.4 %copy.35 = bf16[128,64]{0,1:T(8,128)(2,1)} copy(bf16[128,64]{1,0:T(8,128)(2,1)} %get-tuple-element.33) | data formatting | bytes 32768 | tf_op jit(solution)/shard_map/hand_over/pallas_call | solution.py:701
  (1 shorter events, 0.0 us)
